TPU v7x, 32 devices: a whole 2x2x4 slice. The times are simulated.
32 devices in a mesh: req: 8 (over y, x, core), tp: 4 (over z).
Axes of the slice: x: 2, y: 2, z: 4, core: 2. Of those that a mesh axis runs over, the one named last changes fastest.
Arguments:
- hidden: bfloat16 [8, 384, 3584], P('req'), may hold values from -6 to 6
- embeds: bfloat16 [8, 384, 3584], P('req'), may hold values from -5 to 5
- lengths: int32 [8], P('req'), may hold values from 1 to 384, 1920 in all
- live: int32 [8], P('req'), may hold values 0 or 1
- adapter: int32 [8], P('req'), may hold values from 0 to 3
- incoming_mamba_state: float32 [8, 56, 64, 64], P('req', 'tp'), may hold values from -6 to 6
- mamba_norm_gain: float32 [3584], replicated, may hold values from 0.1 to 1.9
- trainer_gate_input_weight: float32 [3584, 2, 3584], P(('req', 'tp')), may hold values from -0.09375 to 0.09375
- trainer_step_weight: float32 [3584, 184], P(('req', 'tp')), may hold values from -0.09375 to 0.09375
- convolution_inner_taps: float32 [4, 3584], P(None, 'tp'), may hold values from -3 to 3
- convolution_bc_taps: float32 [4, 128], replicated, may hold values from -3 to 3
- step_bias: float32 [56], P('tp'), may hold values from -4 to -0.5
- head_decay_rate: float32 [56], P('tp'), may hold values from 0.05 to 1
- direct_head_term: float32 [56], P('tp'), may hold values from 0.5 to 1.5
- gated_norm_gain: float32 [3584], P('tp'), may hold values from 0.1 to 1.9
- trainer_mamba_output_weight: float32 [3584, 3584], P(None, ('req', 'tp')), may hold values from -0.09375 to 0.09375
- attention_norm_gain: float32 [7168], replicated, may hold values from 0.1 to 1.9
- trainer_query_key_value_weight: float32 [7168, 3, 3584], P(('req', 'tp')), may hold values from -0.33407655 to 0.33407655
- adapter_down_maps: bfloat16 [4, 7168, 128], replicated, may hold values from -0.0625 to 0.0625
- adapter_up_maps: bfloat16 [4, 128, 3, 3584], P(None, None, None, 'tp'), may hold values from -0.5 to 0.5
- trainer_output_weight: float32 [3584, 3584], P(None, ('req', 'tp')), may hold values from -0.09375 to 0.09375
Outputs:
- out_hidden: bfloat16 [8, 384, 3584], P('req', None, 'tp')
- out_state: float32 [8, 56, 64, 64], P('req', 'tp')
Inputs may be any that keep to these rules, and one draw needn't show every extreme that they name: `lengths`: some request has length 384.
All inputs are finite; a program needn't handle non-finite values. No bound on the sum of `lengths` or of `live` on one device may be relied on, other than what follows from the above.
Results may differ from a plain program's by a relative error of at most 0.017.
Values may be sent and summed in bfloat16 or wider, within the bound.
No kernel may reach another device: no remote copies, remote signals or barrier semaphores. Data moves between devices by JAX's collectives and lax.ppermute only.
A program may use at most 384 MiB of HBM per device.

v0:
```python
from functools import partial

import jax
import jax.numpy as jnp
from jax import lax
from jax.experimental import pallas as pl
from jax.experimental.pallas import tpu as pltpu
from jax.sharding import PartitionSpec as P

HS = 224
EPSILON = 1e-05
HIGHEST = lax.Precision.HIGHEST
BF = jnp.bfloat16
F32 = jnp.float32
NT = (((1,), (1,)), ((), ()))
NN = (((1,), (0,)), ((), ()))
TN = (((0,), (0,)), ((), ()))
MB = 1 << 20


def dot(a, b, dims=NN, precision=None):
    return lax.dot_general(a, b, dims, precision=precision, preferred_element_type=F32)


def params(mb):
    return pltpu.CompilerParams(vmem_limit_bytes=mb * MB)


def cost(flops, nbytes):
    return pl.CostEstimate(flops=flops, bytes_accessed=nbytes, transcendentals=0)


def exchange(value, axis, bits):
    count = lax.axis_size(axis)
    return lax.ppermute(value, axis, [(i, i ^ bits) for i in range(count)])


def after(values, waited):
    held = lax.optimization_barrier(tuple(values) + tuple(waited))
    return list(held[: len(values)])


def prepare_input_kernel(idx_ref, w_ref, small_ref, *outs):
    tp = idx_ref[1]
    count = len(outs)
    share = w_ref.shape[2] // count
    for k in range(2):
        for t in range(count):
            piece = w_ref[k, :, t * share : (t + 1) * share].astype(BF)
            for b in range(count):

                @pl.when(tp ^ b == t)
                def _():
                    outs[b][:, k * share : (k + 1) * share] = piece

    for b in range(count):
        outs[b][:, 2 * share :] = small_ref[...]


def prepare_input(idx, weight, small, count):
    _, rows, width = weight.shape
    cols = 2 * width // count + small.shape[1]
    vm = pl.BlockSpec(memory_space=pltpu.VMEM)
    outs = pl.pallas_call(
        prepare_input_kernel,
        in_specs=[pl.BlockSpec(memory_space=pltpu.SMEM), vm, vm],
        out_specs=(vm,) * count,
        out_shape=(jax.ShapeDtypeStruct((rows, cols), BF),) * count,
        compiler_params=params(32),
        cost_estimate=cost(10**6, 6 * MB),
        name="prepare_input",
    )(idx, weight, small)
    return list(outs)


def prepare_kernel(groups, w_ref, *outs):
    for out_ref, parts in zip(outs, groups):
        count = out_ref.shape[0]
        share = w_ref.shape[2] // count
        for j, k in enumerate(parts):
            for t in range(count):
                piece = w_ref[k, :, t * share : (t + 1) * share].astype(BF)
                out_ref[t, :, j * share : (j + 1) * share] = piece


def prepare(weight, count, groups):
    parts, rows, width = weight.shape
    share = width // count
    block = rows // 2 if rows % 32 == 0 else rows
    shapes = [jax.ShapeDtypeStruct((count, rows, share * len(g)), BF) for g in groups]
    return pl.pallas_call(
        partial(prepare_kernel, groups),
        grid=(rows // block,),
        in_specs=[pl.BlockSpec((parts, block, width), lambda i: (0, i, 0))],
        out_specs=tuple(pl.BlockSpec((count, block, v.shape[2]), lambda i: (0, i, 0)) for v in shapes),
        out_shape=tuple(shapes),
        compiler_params=params(40),
        cost_estimate=cost(10**6, parts * rows * width * 6),
        name="prepare",
    )(weight)


def tp_trade(slices):
    out = lax.all_to_all(slices, "tp", split_axis=0, concat_axis=0, tiled=True)
    return out.reshape(-1, slices.shape[2])


def norm_kernel(x_ref, gain_ref, out_ref):
    depth = out_ref.shape[2]
    x = x_ref[...].astype(F32)
    scale = lax.rsqrt(jnp.mean(x * x, axis=1, keepdims=True) + EPSILON)
    for i in range(out_ref.shape[0]):
        span = slice(i * depth, (i + 1) * depth)
        out_ref[i] = (x_ref[:, span].astype(F32) * scale * gain_ref[:, span]).astype(BF)


def norm(x, gain, owners):
    tokens, width = x.shape
    vm = pl.BlockSpec(memory_space=pltpu.VMEM)
    return pl.pallas_call(
        norm_kernel,
        in_specs=[vm, vm],
        out_specs=vm,
        out_shape=jax.ShapeDtypeStruct((owners, tokens, width // owners), BF),
        compiler_params=params(32),
        cost_estimate=cost(10**7, 6 * MB),
        name="norm",
    )(x, gain)


def tp_send(pieces):
    return [pieces[0]] + [exchange(p, "tp", b) for b, p in enumerate(pieces) if b]


def by_xor(slices):
    me = lax.axis_index("tp")
    return [
        lax.dynamic_index_in_dim(slices, me ^ b, 0, keepdims=False) for b in range(slices.shape[0])
    ]


def place_kernel(idx_ref, *refs):
    out_ref = refs[-1]
    rows = refs[0].shape[0]
    for b, ref in enumerate(refs[:-1]):
        out_ref[pl.ds(pl.multiple_of((idx_ref[1] ^ b) * rows, 16), rows), :] = ref[...]


def tp_place(idx, received):
    count = len(received)
    rows, cols = received[0].shape
    if rows % 16:
        out = jnp.zeros((count, rows, cols), BF)
        for b, piece in enumerate(received):
            out = lax.dynamic_update_index_in_dim(out, piece, idx[1] ^ b, 0)
        return out.reshape(count * rows, cols)
    vm = pl.BlockSpec(memory_space=pltpu.VMEM)
    return pl.pallas_call(
        place_kernel,
        in_specs=[pl.BlockSpec(memory_space=pltpu.SMEM)] + [vm] * count,
        out_specs=vm,
        out_shape=jax.ShapeDtypeStruct((count * rows, cols), BF),
        compiler_params=params(24),
        cost_estimate=cost(10**6, 2 * count * rows * cols * 2),
        name="place",
    )(idx, *received)


def gather_rows(piece):
    return lax.all_gather(piece, "req", axis=0, tiled=True)


class Gather:
    def __init__(self, own):
        self.own = own
        self.count = lax.axis_size("req")
        self.pieces = [(0, 0, own)]

    def first(self):
        own = self.own
        if self.count == 8:
            self.px, self.py = exchange(own, "req", 2), exchange(own, "req", 4)
            return [self.px, self.py]
        moved = [(0, own)]
        bit = 2
        while bit < self.count:
            moved = moved + [(at ^ bit, exchange(v, "req", bit)) for at, v in moved]
            bit *= 2
        self.moved = moved
        return [v for _, v in moved[1:]]

    def second(self):
        if self.count != 8:
            self.pieces = [(at, 0, v) for at, v in self.moved]
            self.pieces += [(at ^ 1, 0, exchange(v, "req", 1)) for at, v in self.moved]
            return []
        half = -(-self.own.shape[0] // 32) * 16
        self.half = half
        self.d0 = exchange(self.py[:half], "req", 2)
        self.d1 = exchange(self.px[half:], "req", 4)
        self.pieces.append((1, 0, exchange(self.own, "req", 1)))
        self.pieces += [(2, 0, self.px), (4, 0, self.py)]
        self.pieces += [(3, 0, exchange(self.px, "req", 1)), (5, 0, exchange(self.py, "req", 1))]
        return [self.d0, self.d1]

    def third(self):
        if self.count != 8:
            return
        self.pieces += [(6, 0, self.d0), (6, self.half, self.d1)]
        self.pieces += [
            (7, 0, exchange(self.d0, "req", 1)),
            (7, self.half, exchange(self.d1, "req", 1)),
        ]

    def refresh(self, names, values):
        for name, value in zip(names, values):
            setattr(self, name, value)


def pieces_kernel(places, req_ref, act_ref, *refs):
    count = len(places)
    out_ref, buf_ref, acc_ref, sems = refs[count:]
    me = req_ref[0]
    width = acc_ref.shape[1]
    starts = []
    total = 0
    for _, _, rows in places:
        starts.append(total)
        total += rows

    def copy(i):
        rows = places[i][2]
        return pltpu.make_async_copy(
            refs[i], buf_ref.at[starts[i] : starts[i] + rows, :], sems.at[i]
        )

    for i in range(count):
        copy(i).start()
    for i, (at, low, rows) in enumerate(places):
        copy(i).wait()
        a = act_ref[me ^ at][:, low : low + rows]
        for left in range(0, width, 512):
            span = slice(left, min(left + 512, width))
            part = dot(a, buf_ref[starts[i] : starts[i] + rows, span])
            if i:
                part = part + acc_ref[:, span]
            if i < count - 1:
                acc_ref[:, span] = part
            else:
                out_ref[:, span] = part.astype(BF)


def pieces_matmul(act, gathered):
    owners, tokens, depth = act.shape
    width = gathered.own.shape[1]
    me = lax.axis_index("req").astype(jnp.int32).reshape(1)
    places = [(at, first, v.shape[0]) for at, first, v in gathered.pieces]
    arrays = [v for _, _, v in gathered.pieces]
    vm = pl.BlockSpec(memory_space=pltpu.VMEM)
    return pl.pallas_call(
        partial(pieces_kernel, places),
        in_specs=[pl.BlockSpec(memory_space=pltpu.SMEM), vm]
        + [pl.BlockSpec(memory_space=pl.ANY)] * len(arrays),
        out_specs=vm,
        out_shape=jax.ShapeDtypeStruct((tokens, width), BF),
        scratch_shapes=[
            pltpu.VMEM((owners * depth, width), BF),
            pltpu.VMEM((tokens, width), F32),
            pltpu.SemaphoreType.DMA((len(arrays),)),
        ],
        compiler_params=params(40),
        cost_estimate=cost(2 * owners * tokens * depth * width, owners * depth * width * 2),
        name="zx",
    )(me, act, *arrays)


def rows_kernel(act_ref, w_ref, low_ref, up_ref, out_ref, acc_ref):
    step = pl.program_id(0)
    part = dot(act_ref[0], w_ref[...])

    @pl.when(step == 0)
    def _():
        acc_ref[...] = part + dot(low_ref[...], up_ref[...])

    @pl.when((step > 0) & (step < pl.num_programs(0) - 1))
    def _():
        acc_ref[...] += part

    @pl.when(step == pl.num_programs(0) - 1)
    def _():
        out_ref[...] = (acc_ref[...] + part).astype(BF)


def rows_matmul(act, weight, low, up):
    owners, tokens, depth = act.shape
    width = weight.shape[1]
    return pl.pallas_call(
        rows_kernel,
        grid=(owners,),
        in_specs=[
            pl.BlockSpec((1, tokens, depth), lambda i: (i, 0, 0)),
            pl.BlockSpec((depth, width), lambda i: (i, 0)),
            pl.BlockSpec(low.shape, lambda i: (0, 0)),
            pl.BlockSpec(up.shape, lambda i: (0, 0)),
        ],
        out_specs=pl.BlockSpec((tokens, width), lambda i: (0, 0)),
        out_shape=jax.ShapeDtypeStruct((tokens, width), BF),
        scratch_shapes=[pltpu.VMEM((tokens, width), F32)],
        compiler_params=params(58),
        cost_estimate=cost(2 * owners * tokens * depth * width, owners * depth * width * 2),
        name="qkv",
    )(act, weight, low, up)


def scan_kernel(
    heads, inner, state_dim, chunk, info_ref, zx_ref, taps_ref, bc_taps_ref, bias_ref, bias_t_ref,
    rate_ref, rate_t_ref, direct_ref, out_ref, final_ref, pad_ref, bcpad_ref, conv_ref, bc_ref,
):
    tokens = out_ref.shape[0]
    head_dim = inner // heads
    length, first_head = info_ref[0], info_ref[1]
    width = taps_ref.shape[0]
    pad_ref[0:8, :] = jnp.zeros((8, inner), F32)
    pad_ref[8:, :] = zx_ref[:, inner : 2 * inner].astype(F32)
    bcpad_ref[0:8, :] = jnp.zeros((8, 2 * state_dim), F32)
    bcpad_ref[8:, :] = zx_ref[:, 2 * inner : 2 * inner + 2 * state_dim].astype(F32)
    for base in range(0, tokens, chunk):
        x = jnp.zeros((chunk, inner), F32)
        b = jnp.zeros((chunk, 2 * state_dim), F32)
        for k in range(width):
            low = base + 8 - (width - 1) + k
            x = x + taps_ref[k : k + 1, :] * pad_ref[low : low + chunk, :]
            b = b + bc_taps_ref[k : k + 1, :] * bcpad_ref[low : low + chunk, :]
        conv_ref[base : base + chunk, :] = x * jax.nn.sigmoid(x)
        bc_ref[base : base + chunk, :] = b * jax.nn.sigmoid(b)

    def softplus(v):
        return jnp.maximum(v, 0.0) + jnp.log1p(jnp.exp(-jnp.abs(v)))

    raw = zx_ref[:, 2 * inner + 2 * state_dim :]
    lanes = raw.shape[1]
    pick = (
        lax.broadcasted_iota(jnp.int32, (lanes, 128), 0)
        == lax.broadcasted_iota(jnp.int32, (lanes, 128), 1) + first_head
    ).astype(F32).astype(BF)
    pick_t = (
        lax.broadcasted_iota(jnp.int32, (16, lanes), 1)
        == lax.broadcasted_iota(jnp.int32, (16, lanes), 0) + first_head
    ).astype(F32).astype(BF)
    valid = lax.broadcasted_iota(jnp.int32, (tokens, 128), 0) < length
    valid_t = lax.broadcasted_iota(jnp.int32, (16, tokens), 1) < length
    steps = jnp.where(valid, softplus(dot(raw, pick) + bias_ref[...]), 0.0)
    steps_t = jnp.where(valid_t, softplus(dot(pick_t, raw, NT) + bias_t_ref[...]), 0.0)
    logs = -steps * rate_ref[...]
    logs_t = -steps_t * rate_t_ref[...]
    rows = lax.broadcasted_iota(jnp.int32, (chunk, chunk), 0)
    cols = lax.broadcasted_iota(jnp.int32, (chunk, chunk), 1)
    lower = rows >= cols
    tri = lower.astype(F32)
    tri_t = (rows <= cols).astype(F32)
    spread = (
        lax.broadcasted_iota(jnp.int32, (128, inner), 1) // head_dim
        == lax.broadcasted_iota(jnp.int32, (128, inner), 0)
    ).astype(F32)
    state = jnp.zeros((state_dim, inner), F32)
    for base in range(0, tokens, chunk):
        span = slice(base, base + chunk)
        x = conv_ref[span, :]
        bc = bc_ref[span, :]
        b_rows = bc[:, :state_dim].astype(BF)
        c_rows = bc[:, state_dim:].astype(BF)
        cumul = dot(tri, logs[span, :], precision=HIGHEST)
        cumul_t = dot(logs_t[:, span], tri_t, precision=HIGHEST)
        last = cumul[chunk - 1 : chunk, :]
        near = dot(c_rows, b_rows, NT)
        near = jnp.where(lower, near, 0.0)
        grown = dot(jnp.exp(cumul), spread, precision=HIGHEST)
        x_dt = x * dot(steps[span, :], spread, precision=HIGHEST)
        tail = dot(jnp.exp(last - cumul), spread, precision=HIGHEST)
        carried = dot(c_rows, state.astype(BF)) * grown
        x_dt_b = x_dt.astype(BF)
        direct = direct_ref[...] * x + carried
        gate = zx_ref[span, :inner].astype(F32)
        gate = gate * jax.nn.sigmoid(gate)
        per = 128 // head_dim
        for tile in range(pl.cdiv(heads, per)):
            left, right = tile * 128, min(tile * 128 + 128, inner)
            lane = lax.broadcasted_iota(jnp.int32, (chunk, right - left), 1)
            within = jnp.zeros((chunk, right - left), F32)
            for h in range(tile * per, min(tile * per + per, heads)):
                gap = cumul[:, h : h + 1] - cumul_t[h : h + 1, :]
                gap = jnp.where(lower, gap, -1e30)
                weights = (near * jnp.exp(gap)).astype(BF)
                part = dot(weights, x_dt_b[:, left:right])
                mine = lane // head_dim == h - tile * per
                within = jnp.where(mine, part, within)
            y = (within + direct[:, left:right]) * gate[:, left:right]
            out_ref[span, left:right] = y.astype(BF)
        fresh = dot(b_rows, (x_dt * tail).astype(BF), TN)
        kept = dot(jnp.broadcast_to(jnp.exp(last), (8, 128)), spread, precision=HIGHEST)[0:1, :]
        state = state * kept + fresh
    final_ref[...] = state.T


def head_rows(bias, rate, direct, heads, inner):
    def padded(v):
        return [
            jnp.pad(v[None, :], ((0, 0), (0, 128 - heads))),
            jnp.pad(v[:, None], ((0, 16 - heads), (0, 0))),
        ]

    return padded(bias) + padded(rate) + [jnp.repeat(direct, inner // heads)[None, :]]


def run_scan(zx, info, taps, bc_taps, per_head, heads, inner, state_dim):
    tokens = zx.shape[0]
    vm = pl.BlockSpec(memory_space=pltpu.VMEM)
    return pl.pallas_call(
        partial(scan_kernel, heads, inner, state_dim, 128),
        in_specs=[pl.BlockSpec(memory_space=pltpu.SMEM)] + [vm] * 8,
        out_specs=(vm, vm),
        out_shape=(
            jax.ShapeDtypeStruct((tokens, inner), BF),
            jax.ShapeDtypeStruct((inner, state_dim), F32),
        ),
        scratch_shapes=[
            pltpu.VMEM((tokens + 8, inner), F32),
            pltpu.VMEM((tokens + 8, 2 * state_dim), F32),
            pltpu.VMEM((tokens, inner), F32),
            pltpu.VMEM((tokens, 2 * state_dim), F32),
        ],
        compiler_params=params(40),
        cost_estimate=cost(6 * 10**9, 4 * MB),
        name="scan",
    )(info, zx, taps, bc_taps, *per_head)


def column_weights(gathered, which):
    owners, _, rows, width = gathered.shape
    if rows % 16:
        gathered = gathered[:, which].reshape(1, 1, owners * rows, width)
        which = 0
    block = (gathered.shape[0], 1) + gathered.shape[2:]
    return gathered, pl.BlockSpec(block, lambda i, x: (0, which, 0, 0))


def columns_kernel(tp_count, ordered, scaled, idx_ref, *refs):
    a_refs, gain_ref, stream_ref, w_ref, out_ref = refs[:tp_count], *refs[tp_count:]
    tp = 0 if ordered else idx_ref[1]
    tokens, share = a_refs[0].shape
    rows = out_ref.shape[0]
    squares = jnp.zeros((tokens, 1), F32)
    total = None
    for b in range(tp_count):
        act = a_refs[b][...]
        if scaled:
            raw = act.astype(F32)
            squares = squares + jnp.sum(raw * raw, axis=1, keepdims=True)
            act = (raw * gain_ref[tp ^ b]).astype(BF)
        if ordered:
            weights = w_ref[:, 0, :, b * share : (b + 1) * share]
        else:
            weights = w_ref[:, 0, :, pl.ds(pl.multiple_of((tp ^ b) * share, 128), share)]
        part = dot(weights.reshape(rows, share), act, NT)
        total = part if total is None else total + part
    if scaled:
        scale = lax.rsqrt(squares / (share * tp_count) + EPSILON)
        total = total * jnp.broadcast_to(scale, (tokens, 128)).T[0:1, :]
        out_ref[...] = (stream_ref[...].astype(F32) + total).astype(BF)
    else:
        total = stream_ref[...].astype(F32) + total
        place = lax.broadcasted_iota(jnp.int32, total.shape, 1)
        keep = place < jnp.where(idx_ref[3] > 0, idx_ref[2], 0)
        out_ref[...] = jnp.where(keep, total, 0.0).astype(BF)


def columns(gathered, which, idx, parts, gain, stream, scaled):
    ordered = parts[0].shape[1] % 128 != 0
    if ordered:
        stacked = jnp.stack(parts)
        for b, part in enumerate(parts):
            stacked = lax.dynamic_update_index_in_dim(stacked, part, idx[1] ^ b, 0)
        parts = [stacked[i] for i in range(len(parts))]
    weights, spec = column_weights(gathered, which)

    def full(v):
        return pl.BlockSpec(v.shape, lambda i, x: (0,) * v.ndim)

    return pl.pallas_call(
        partial(columns_kernel, len(parts), ordered, scaled),
        grid_spec=pltpu.PrefetchScalarGridSpec(
            num_scalar_prefetch=1,
            grid=(1,),
            in_specs=[full(v) for v in parts] + [full(gain), full(stream), spec],
            out_specs=full(stream),
        ),
        out_shape=jax.ShapeDtypeStruct(stream.shape, BF),
        compiler_params=params(58),
        cost_estimate=cost(2 * 896 * 384 * 3584, 12 * MB),
        name="mixer" if scaled else "output",
    )(idx, *parts, gain, stream, weights)


def join_kernel(which_ref, mid_ref, embeds_ref, gain_ref, down_ref, act_ref, low_ref):
    owners, tokens, depth = act_ref.shape
    half = owners // 2
    squares = jnp.zeros((tokens, 1), F32)
    for i in range(owners):
        if i < half:
            part = mid_ref[i * depth : (i + 1) * depth, :].astype(F32).T
        else:
            part = embeds_ref[:, (i - half) * depth : (i - half + 1) * depth].astype(F32)
        squares = squares + jnp.sum(part * part, axis=1, keepdims=True)
        act_ref[i] = part.astype(BF)
    scale = lax.rsqrt(squares / (owners * depth) + EPSILON)
    low = jnp.zeros((tokens, down_ref.shape[2]), F32)
    for i in range(owners):
        gain = gain_ref[:, i * depth : (i + 1) * depth]
        value = (act_ref[i].astype(F32) * scale * gain).astype(BF)
        act_ref[i] = value
        low = low + dot(value, down_ref[0, i * depth : (i + 1) * depth, :])
    low_ref[...] = low.astype(BF)


def join(mid, embeds, gain, down, which, owners):
    width, tokens = mid.shape
    depth = 2 * width // owners
    rank = down.shape[2]
    return pl.pallas_call(
        join_kernel,
        grid_spec=pltpu.PrefetchScalarGridSpec(
            num_scalar_prefetch=1,
            grid=(1,),
            in_specs=[
                pl.BlockSpec((width, tokens), lambda i, a: (0, 0)),
                pl.BlockSpec((tokens, width), lambda i, a: (0, 0)),
                pl.BlockSpec((1, 2 * width), lambda i, a: (0, 0)),
                pl.BlockSpec((1, 2 * width, rank), lambda i, a: (a[0], 0, 0)),
            ],
            out_specs=(
                pl.BlockSpec((owners, tokens, depth), lambda i, a: (0, 0, 0)),
                pl.BlockSpec((tokens, rank), lambda i, a: (0, 0)),
            ),
        ),
        out_shape=(
            jax.ShapeDtypeStruct((owners, tokens, depth), BF),
            jax.ShapeDtypeStruct((tokens, rank), BF),
        ),
        compiler_params=params(48),
        cost_estimate=cost(2 * 7168 * 384 * 128, 13 * MB),
        name="join",
    )(which, mid, embeds, gain, down)


def attend_kernel(heads, size, info_ref, q_ref, kv_ref, out_ref):
    tokens, width = q_ref.shape
    length = info_ref[0]
    rows = lax.broadcasted_iota(jnp.int32, (tokens, tokens), 0)
    cols = lax.broadcasted_iota(jnp.int32, (tokens, tokens), 1)
    allowed = (cols <= rows) & (cols < length)
    spans = []
    for h in range(heads):
        left = h * size // 128 * 128
        right = min(-(-(h + 1) * size // 128) * 128, width)
        spans.append((left, right))
    done = {}
    for h, (left, right) in enumerate(spans):
        lane = lax.broadcasted_iota(jnp.int32, (tokens, right - left), 1) + left
        mine = (lane >= h * size) & (lane < (h + 1) * size)
        query = jnp.where(mine, q_ref[:, left:right].astype(F32), 0.0).astype(BF)
        scores = dot(query, kv_ref[:, left:right], NT) * size ** (-0.5)
        scores = jnp.where(allowed, scores, -1e30)
        peak = jnp.max(scores, axis=1, keepdims=True)
        expo = jnp.exp(scores - peak)
        weights = (expo / jnp.sum(expo, axis=1, keepdims=True)).astype(BF)
        mixed = dot(weights, kv_ref[:, width + left : width + right])
        mixed = jnp.where(mine, mixed, 0.0)
        for at in range(left, right, 128):
            to = min(at + 128, right)
            part = mixed[:, at - left : to - left]
            done[at] = part if at not in done else done[at] + part
    for at, value in done.items():
        out_ref[:, at : at + value.shape[1]] = value.astype(BF)


def attend(q, kv, info, heads):
    vm = pl.BlockSpec(memory_space=pltpu.VMEM)
    return pl.pallas_call(
        partial(attend_kernel, heads, HS),
        in_specs=[pl.BlockSpec(memory_space=pltpu.SMEM), vm, vm],
        out_specs=vm,
        out_shape=jax.ShapeDtypeStruct(q.shape, BF),
        compiler_params=params(40),
        cost_estimate=cost(6 * 10**9, 3 * MB),
        name="attend",
    )(info, q, kv)


def finish_kernel(rows, idx_ref, *refs):
    out_ref, all_ref = refs[-2:]
    count = len(refs) - 2
    groups = refs[0].shape[0] // rows
    for g in range(groups):
        for b, ref in enumerate(refs[:-2]):
            to = pl.multiple_of((g * count + (idx_ref[1] ^ b)) * rows, 16)
            all_ref[pl.ds(to, rows), :] = ref[g * rows : (g + 1) * rows, :]
    out_ref[...] = all_ref[...].astype(F32).T.astype(BF)


def finish(idx, parts, rows):
    count = len(parts)
    tokens = parts[0].shape[1]
    if rows % 16:
        out = jnp.zeros((parts[0].shape[0] // rows, count, rows, tokens), BF)
        for b, part in enumerate(parts):
            part = part.reshape(-1, 1, rows, tokens)
            out = lax.dynamic_update_slice_in_dim(out, part, idx[1] ^ b, 1)
        return out.reshape(-1, tokens).T
    vm = pl.BlockSpec(memory_space=pltpu.VMEM)
    width = count * parts[0].shape[0]
    return pl.pallas_call(
        partial(finish_kernel, rows),
        in_specs=[pl.BlockSpec(memory_space=pltpu.SMEM)] + [vm] * count,
        out_specs=vm,
        out_shape=jax.ShapeDtypeStruct((tokens, width), BF),
        scratch_shapes=[pltpu.VMEM((width, tokens), BF)],
        compiler_params=params(24),
        cost_estimate=cost(10**6, 2 * MB),
        name="finish",
    )(idx, *parts)


def local(
    hidden,
    embeds,
    lengths,
    live,
    adapter,
    incoming_mamba_state,
    mamba_norm_gain,
    trainer_gate_input_weight,
    trainer_step_weight,
    convolution_inner_taps,
    convolution_bc_taps,
    step_bias,
    head_decay_rate,
    direct_head_term,
    gated_norm_gain,
    trainer_mamba_output_weight,
    attention_norm_gain,
    trainer_query_key_value_weight,
    adapter_down_maps,
    adapter_up_maps,
    trainer_output_weight,
):
    tp_count, req_count = lax.axis_size("tp"), lax.axis_size("req")
    tp_index = lax.axis_index("tp").astype(jnp.int32)
    req_index = lax.axis_index("req").astype(jnp.int32)
    idx = jnp.stack([req_index, tp_index, lengths[0], live[0]])
    _, seq_len, width = hidden.shape
    heads = step_bias.shape[0]
    inner = convolution_inner_taps.shape[1]
    state_dim = convolution_bc_taps.shape[1] // 2
    rows = trainer_gate_input_weight.shape[0]

    small = trainer_step_weight.astype(BF)
    high = lax.optimization_barrier(gated_norm_gain.astype(BF))
    rest = (gated_norm_gain - high.astype(F32)).astype(BF)
    small = jnp.concatenate([small, high.reshape(rows, -1), rest.reshape(rows, -1)], axis=1)
    used, each = trainer_step_weight.shape[1], inner // rows
    small = jnp.pad(small, ((0, 0), (0, 256 - small.shape[1])))
    zx_send = prepare_input(idx, trainer_gate_input_weight.transpose(1, 0, 2), small, tp_count)
    zx_received = tp_send(zx_send)
    o_pair = jnp.stack([trainer_mamba_output_weight.astype(BF).T, trainer_output_weight.astype(BF).T])
    o_pair = gather_rows(o_pair[None])
    q_send, kv_send = prepare(
        trainer_query_key_value_weight.transpose(1, 0, 2), tp_count, [(0,), (1, 2)]
    )
    normed_in = norm(hidden[0], mamba_norm_gain[None, :], req_count)
    per_head = head_rows(step_bias, head_decay_rate, direct_head_term, heads, inner)
    zx_own = tp_place(idx, zx_received)

    zx_own, q_send, *_ = after([zx_own, q_send], [normed_in] + per_head)
    zx_gather = Gather(zx_own)
    zx_first = zx_gather.first()
    q_own = tp_trade(q_send)
    stream_t = hidden[0].T.reshape(req_count, tp_count, rows, seq_len)
    stream_t = lax.dynamic_index_in_dim(stream_t, tp_index, 1, keepdims=False)
    stream_t = stream_t.reshape(req_count * rows, seq_len)
    ups = lax.dynamic_index_in_dim(adapter_up_maps, adapter[0], 0, keepdims=False)
    ups = [ups[:, 0], ups[:, 1:].reshape(ups.shape[0], -1)]
    gain_all = zx_own.reshape(tp_count, rows, -1)[:, :, 2 * inner + used :].astype(F32)
    gain_all = (gain_all[:, :, :each] + gain_all[:, :, each : 2 * each]).reshape(tp_count, 1, inner)

    held = after(zx_first + [kv_send, q_own], [stream_t, gain_all] + ups)
    if req_count == 8:
        zx_gather.refresh(["px", "py"], held[:2])
    kv_send, q_own = held[-2:]
    q_server = gather_rows(q_own)
    zx_second = zx_gather.second()
    kv_own = tp_trade(kv_send)
    zx_gather.third()

    zx = pieces_matmul(normed_in, zx_gather)
    info = jnp.stack([lengths[0], tp_index * heads])
    raw, final = run_scan(
        zx, info, convolution_inner_taps, convolution_bc_taps, per_head, heads, inner, state_dim
    )
    raw, kv_own = after([raw, kv_own], [])
    kv_server = gather_rows(kv_own)
    raws = tp_send([raw] * tp_count)
    mid_own = columns(o_pair, 0, idx, raws, gain_all, stream_t, True)
    mids = jnp.zeros((tp_count,) + mid_own.shape, BF)
    for b, moved in enumerate(tp_send([mid_own] * tp_count)):
        mids = lax.dynamic_update_index_in_dim(mids, moved, tp_index ^ b, 0)
    mid = mids.reshape(tp_count, req_count, rows, seq_len).transpose(1, 0, 2, 3)
    mid = mid.reshape(width, seq_len)
    act, low = join(mid, embeds[0], attention_norm_gain[None, :], adapter_down_maps, adapter, 4)
    queries = rows_matmul(act, q_server, low, ups[0])
    keys_values = rows_matmul(act, kv_server, low, ups[1])
    attended = attend(queries, keys_values, lengths, queries.shape[1] // HS)
    whole = tp_send([attended] * tp_count)
    result = columns(o_pair, 1, idx, whole, gain_all, mid_own, False)
    result = tp_send(by_xor(result.reshape(tp_count, -1, seq_len)))
    result = finish(idx, result, rows)
    final = final.reshape((1, heads, inner // heads, state_dim))
    state = jnp.where((live > 0)[:, None, None, None], final, incoming_mamba_state)
    return (result[None], state)


def solution(mesh):
    placed = (
        P("req", None, None),
        P("req", None, None),
        P("req"),
        P("req"),
        P("req"),
        P("req", "tp", None, None),
        P(),
        P(("req", "tp"), None, None),
        P(("req", "tp"), None),
        P(None, "tp"),
        P(),
        P("tp"),
        P("tp"),
        P("tp"),
        P("tp"),
        P(None, ("req", "tp")),
        P(),
        P(("req", "tp"), None, None),
        P(),
        P(None, None, None, "tp"),
        P(None, ("req", "tp")),
    )
    return jax.shard_map(
        local,
        mesh=mesh,
        in_specs=placed,
        out_specs=(P("req", None, "tp"), P("req", "tp", None, None)),
        check_vma=False,
    )
```

profile of v0, /device:TPU:0, one launch (start us, length us, event | category | flops | bytes accessed | tf_op | source)
XLA Modules:
  0.0 465.7 jit_solution(18220978468392985647)
XLA Ops:
  7.2 2.2 convert_bitcast_fusion
  12.1 4.2 copy.58
  16.9 1.9 copy-done.2
  18.8 2.0 prepare_input.1
  20.8 3.0 collective-permute-start
  23.8 2.7 collective-permute-start.1
  26.9 3.7 copy-done.4
  34.4 1.6 copy-done.6
  36.0 7.7 %collective-permute-done.refs_1_ = bf16[112,2048]{1,0:T(8,128)(2,1)} collective-permute-done((bf16[112,2048]{1,0:T(8,128)(2,1)}, bf16[112,2048]{1,0:T(8,128)(2,1)}, u32[]{:S(2)}, u32[]{:S(2)}) %collective-permute-start) | collective-permute-done | bytes 458784 | tf_op jit(solution)/shard_map/ppermute | solution.py:35
  43.7 14.4 %collective-permute-done.1.refs_2_ = bf16[112,2048]{1,0:T(8,128)(2,1)} collective-permute-done((bf16[112,2048]{1,0:T(8,128)(2,1)}, bf16[112,2048]{1,0:T(8,128)(2,1)}, u32[]{:S(2)}, u32[]{:S(2)}) %collective-permute-start.1) | collective-permute-done | bytes 458784 | tf_op jit(solution)/shard_map/ppermute | solution.py:35
  60.8 11.2 %all-to-all-start = ((bf16[4,224,896]{2,1,0:T(8,128)(2,1)}), bf16[4,224,896]{2,1,0:T(8,128)(2,1)}, u32[]{:S(2)}, u32[]{:S(2)}) async-start(bf16[4,224,896]{2,1,0:T(8,128)(2,1)} %copy-done.11), calls=%async_computation | async-start | bytes 3211264 | tf_op jit(solution)/shard_map/all_to_all | solution.py:104
  73.6 1.5 collective-permute-start.5
  75.7 4.5 copy.51
  82.1 2.0 constant_dynamic-slice_fusion
  84.1 1.6 slice_bitcast_fusion.1.up_ref
  86.1 37.9 %collective-permute-done.4.refs_2_ = bf16[448,2048]{1,0:T(8,128)(2,1)} collective-permute-done((bf16[448,2048]{1,0:T(8,128)(2,1)}, bf16[448,2048]{1,0:T(8,128)(2,1)}, u32[]{:S(2)}, u32[]{:S(2)}) %collective-permute-start.4) | collective-permute-done | bytes 1835040 | tf_op jit(solution)/shard_map/ppermute | solution.py:35
  124.0 4.7 %all-to-all-start.1 = ((bf16[4,224,1792]{2,1,0:T(8,128)(2,1)}), bf16[4,224,1792]{2,1,0:T(8,128)(2,1)}, u32[]{:S(2)}, u32[]{:S(2)}) async-start(bf16[4,224,1792]{2,1,0:T(8,128)(2,1)} %copy-done.5), calls=%async_computation.1 | async-start | bytes 6422528 | tf_op jit(solution)/shard_map/all_to_all | solution.py:104
  134.2 36.4 %collective-permute-done.8.refs_6_ = bf16[224,2048]{1,0:T(8,128)(2,1)S(1)} collective-permute-done((bf16[224,2048]{1,0:T(8,128)(2,1)S(1)}, bf16[224,2048]{1,0:T(8,128)(2,1)S(1)}, u32[]{:S(2)}, u32[]{:S(2)}) %collective-permute-start.8) | collective-permute-done | bytes 917536 | tf_op jit(solution)/shard_map/ppermute | solution.py:35
  170.7 2.1 collective-permute-done.9.refs_7_
  173.3 2.3 collective-permute-done.11.refs_9_
  175.6 2.0 copy-done.10
  177.7 10.8 %zx.1.zx_ref = bf16[384,2048]{1,0:T(8,128)(2,1)S(1)} custom-call(s32[1]{0:T(128)} %bitcast.req_ref, bf16[8,384,448]{2,1,0:T(8,128)(2,1)} %copy-done.6, bf16[448,2048]{1,0:T(8,128)(2,1)S(1)} %copy-done.10, bf16[448,2048]{1,0:T(8,128)(2,1)} %collective-permute-done.3.refs_1_, bf16[448,2048]{1,0:T(8,128)(2,1)} %collective-permute-done.4.refs_2_, ...), custom_call_target="tpu_custom_call" | custom-call | flops 5637144576 | bytes 14680064 | tf_op jit(solution)/shard_map/zx/pallas_call | solution.py:260
  188.5 6.4 %scan.1 = (bf16[384,896]{1,0:T(8,128)(2,1)S(1)}, f32[896,64]{1,0:T(8,128)S(1)}) custom-call(s32[2]{0:T(128)S(1)} %pad_add_fusion.1.info_ref, bf16[384,2048]{1,0:T(8,128)(2,1)S(1)} %zx.1.zx_ref, f32[4,896]{1,0:T(4,128)S(1)} %copy-done.19, f32[4,128]{1,0:T(4,128)S(1)} %copy-done.20, f32[1,128]{1,0:T(1,128)S(1)} %pad.19.bias_ref, f32[16,1]{1,0:T(8,128)S(1)} %pad.20.bias_t_ref, ...), custom_call_target="tpu_custom_call" | custom-call | flops 6000000000 | bytes 4194304 | tf_op jit(solution)/shard_map/scan/pallas_call | solution.py:418
  194.9 5.6 %all-to-all-done.1 = bf16[4,224,1792]{2,1,0:T(8,128)(2,1)} async-done(((bf16[4,224,1792]{2,1,0:T(8,128)(2,1)}), bf16[4,224,1792]{2,1,0:T(8,128)(2,1)}, u32[]{:S(2)}, u32[]{:S(2)}) %all-to-all-start.1) | async-done | bytes 3211296 | tf_op jit(solution)/shard_map/all_to_all | solution.py:104
  200.7 2.0 collective-permute-start.13
  202.7 2.4 collective-permute-start.14
  205.7 25.6 %collective-permute-done.12.refs_1_ = bf16[384,896]{1,0:T(8,128)(2,1)S(1)} collective-permute-done((bf16[384,896]{1,0:T(8,128)(2,1)S(1)}, bf16[384,896]{1,0:T(8,128)(2,1)S(1)}, u32[]{:S(2)}, u32[]{:S(2)}) %collective-permute-start.12) | collective-permute-done | bytes 688160 | tf_op jit(solution)/shard_map/ppermute | solution.py:35
  231.2 18.2 %collective-permute-done.13.refs_2_ = bf16[384,896]{1,0:T(8,128)(2,1)S(1)} collective-permute-done((bf16[384,896]{1,0:T(8,128)(2,1)S(1)}, bf16[384,896]{1,0:T(8,128)(2,1)S(1)}, u32[]{:S(2)}, u32[]{:S(2)}) %collective-permute-start.13) | collective-permute-done | bytes 688160 | tf_op jit(solution)/shard_map/ppermute | solution.py:35
  250.4 9.5 %mixer.1.refs_5_ = bf16[896,384]{1,0:T(8,128)(2,1)} custom-call(s32[4]{0:T(128)} %copy-done.17, bf16[384,896]{1,0:T(8,128)(2,1)} %copy-done.12, bf16[384,896]{1,0:T(8,128)(2,1)} %copy-done.24, bf16[384,896]{1,0:T(8,128)(2,1)} %copy-done.26, bf16[384,896]{1,0:T(8,128)(2,1)} %collective-permute-done.14.refs_3_, f32[4,1,896]{2,1,0:T(1,128)} %copy.53.refs_4_, ...), custom_call_target="tpu_custom_call" | custom-call | flops 2466250752 | bytes 12582912 | tf_op jit(solution)/shard_map/mixer/pallas_call | solution.py:489
  259.9 12.7 %collective-permute-start.15 = (bf16[896,384]{1,0:T(8,128)(2,1)}, bf16[896,384]{1,0:T(8,128)(2,1)S(1)}, u32[]{:S(2)}, u32[]{:S(2)}) collective-permute-start(bf16[896,384]{1,0:T(8,128)(2,1)} %mixer.1.refs_5_), channel_id=1, source_target_pairs={{0,1},{1,0},{2,3},{3,2},{4,5},{5,4},{6,7},{7,6},{8,9},{9,8},{10,11... | collective-permute-start | bytes 2064392 | tf_op jit(solution)/shard_map/ppermute | solution.py:35
  272.6 2.4 collective-permute-start.17
  275.4 23.9 %collective-permute-done.15 = bf16[896,384]{1,0:T(8,128)(2,1)S(1)} collective-permute-done((bf16[896,384]{1,0:T(8,128)(2,1)}, bf16[896,384]{1,0:T(8,128)(2,1)S(1)}, u32[]{:S(2)}, u32[]{:S(2)}) %collective-permute-start.15) | collective-permute-done | bytes 688160 | tf_op jit(solution)/shard_map/ppermute | solution.py:35
  299.4 22.2 %collective-permute-done.16 = bf16[896,384]{1,0:T(8,128)(2,1)S(1)} collective-permute-done((bf16[896,384]{1,0:T(8,128)(2,1)}, bf16[896,384]{1,0:T(8,128)(2,1)S(1)}, u32[]{:S(2)}, u32[]{:S(2)}) %collective-permute-start.16) | collective-permute-done | bytes 688160 | tf_op jit(solution)/shard_map/ppermute | solution.py:35
  323.6 6.9 %join.1 = (bf16[4,384,1792]{2,1,0:T(8,128)(2,1)}, bf16[384,128]{1,0:T(8,128)(2,1)S(1)}) custom-call(s32[1]{0:T(128)} %copy.65.which_ref, bf16[3584,384]{1,0:T(8,128)(2,1)S(1)} %bitcast.68, bf16[384,3584]{1,0:T(8,128)(2,1)S(1)} %bitcast.70, f32[1,7168]{1,0:T(1,128)S(1)} %bitcast.73, bf16[4,7168,128]{2,1,0:T(8,128)(2,1)} %down_ref.1), custom_call_target="tpu_custom_call" | custom-call | flops 704643072 | bytes 13631488 | tf_op jit(solution)/shard_map/join/pallas_call | solution.py:529
  331.1 11.0 %qkv.2.q_ref = bf16[384,896]{1,0:T(8,128)(2,1)} custom-call(bf16[4,384,1792]{2,1,0:T(8,128)(2,1)} %get-tuple-element.33.act_ref, bf16[7168,896]{1,0:T(8,128)(2,1)} %all-gather.5.cloned.1.call-done.w_ref, bf16[384,128]{1,0:T(8,128)(2,1)} %copy-done.15, bf16[128,896]{1,0:T(8,128)(2,1)} %slice_bitcast_fusion.1.up_ref), custom_call_target="tpu_custom_call" | custom-call | flops 4932501504 | bytes 12845056 | tf_op jit(solution)/shard_map/qkv/pallas_call | solution.py:297
  342.2 1.8 all-gather.7.cloned.1.call-done.w_ref
  344.0 16.7 %qkv.3.kv_ref = bf16[384,1792]{1,0:T(8,128)(2,1)} custom-call(bf16[4,384,1792]{2,1,0:T(8,128)(2,1)} %get-tuple-element.33.act_ref, bf16[7168,1792]{1,0:T(8,128)(2,1)} %all-gather.7.cloned.1.call-done.w_ref, bf16[384,128]{1,0:T(8,128)(2,1)} %copy-done.15, bf16[128,1792]{1,0:T(8,128)(2,1)} %bitcast.81), custom_call_target="tpu_custom_call" | custom-call | flops 9865003008 | bytes 25690112 | tf_op jit(solution)/shard_map/qkv/pallas_call | solution.py:297
  362.0 2.4 attend.1.refs_0_
  364.4 10.5 %collective-permute-start.18 = (bf16[384,896]{1,0:T(8,128)(2,1)S(1)}, bf16[384,896]{1,0:T(8,128)(2,1)S(1)}, u32[]{:S(2)}, u32[]{:S(2)}) collective-permute-start(bf16[384,896]{1,0:T(8,128)(2,1)S(1)} %attend.1.refs_0_), channel_id=1, source_target_pairs={{0,1},{1,0},{2,3},{3,2},{4,5},{5,4},{6,7},{7,6},{8,9},{9,8},{10,11... | collective-permute-start | bytes 2064392 | tf_op jit(solution)/shard_map/ppermute | solution.py:35
  375.2 2.1 collective-permute-start.20
  377.3 22.6 %collective-permute-done.18.refs_1_ = bf16[384,896]{1,0:T(8,128)(2,1)S(1)} collective-permute-done((bf16[384,896]{1,0:T(8,128)(2,1)S(1)}, bf16[384,896]{1,0:T(8,128)(2,1)S(1)}, u32[]{:S(2)}, u32[]{:S(2)}) %collective-permute-start.18) | collective-permute-done | bytes 688160 | tf_op jit(solution)/shard_map/ppermute | solution.py:35
  400.0 23.7 %collective-permute-done.19.refs_2_ = bf16[384,896]{1,0:T(8,128)(2,1)S(1)} collective-permute-done((bf16[384,896]{1,0:T(8,128)(2,1)S(1)}, bf16[384,896]{1,0:T(8,128)(2,1)S(1)}, u32[]{:S(2)}, u32[]{:S(2)}) %collective-permute-start.19) | collective-permute-done | bytes 688160 | tf_op jit(solution)/shard_map/ppermute | solution.py:35
  424.5 9.4 %output.1 = bf16[896,384]{1,0:T(8,128)(2,1)} custom-call(s32[4]{0:T(128)} %copy-done.17, bf16[384,896]{1,0:T(8,128)(2,1)} %copy-done.13, bf16[384,896]{1,0:T(8,128)(2,1)} %copy-done.25, bf16[384,896]{1,0:T(8,128)(2,1)} %copy-done.27, bf16[384,896]{1,0:T(8,128)(2,1)} %collective-permute-done.20.refs_3_, f32[4,1,896]{2,1,0:T(1,128)} %copy.53.refs_4_, ...), custom_call_target="tpu_custom_call" | custom-call | flops 2466250752 | bytes 12582912 | tf_op jit(solution)/shard_map/output/pallas_call | solution.py:489
  435.2 10.4 %collective-permute-start.21 = (bf16[224,384]{1,0:T(8,128)(2,1)S(1)}, bf16[224,384]{1,0:T(8,128)(2,1)S(1)}, u32[]{:S(2)}, u32[]{:S(2)}) collective-permute-start(bf16[224,384]{1,0:T(8,128)(2,1)S(1)} %get-tuple-element.40), channel_id=1, source_target_pairs={{0,1},{1,0},{2,3},{3,2},{4,5},{5,4},{6,7},{7,6},{8,9},{9,8},{10,11... | collective-permute-start | bytes 516104 | tf_op jit(solution)/shard_map/ppermute | solution.py:35
  445.6 2.4 collective-permute-start.23
  448.8 3.3 collective-permute-done.21.refs_1_
  452.1 5.3 %collective-permute-done.22.refs_2_ = bf16[224,384]{1,0:T(8,128)(2,1)S(1)} collective-permute-done((bf16[224,384]{1,0:T(8,128)(2,1)S(1)}, bf16[224,384]{1,0:T(8,128)(2,1)S(1)}, u32[]{:S(2)}, u32[]{:S(2)}) %collective-permute-start.22) | collective-permute-done | bytes 172064 | tf_op jit(solution)/shard_map/ppermute | solution.py:35
  457.5 1.7 finish.1
  (137 shorter events, 27.4 us)
Async XLA Ops:
  7.2 73.1 %copy-start = (bf16[4,128,3,896]{3,1,2,0:T(8,128)(2,1)S(1)}, bf16[4,128,3,896]{3,1,2,0:T(8,128)(2,1)}, u32[]{:S(2)}) copy-start(bf16[4,128,3,896]{3,1,2,0:T(8,128)(2,1)} %param.40) | copy-start | bytes 8257540
  7.2 242.3 %all-gather.9.cloned.1.call-start = ((), (), s32[]{:S(2)}) async-start(), calls=%async_computation.4 | async-start | bytes 14450688 | tf_op jit(solution)/shard_map/all_gather | solution.py:170
  12.1 4.5 copy-start.29
  16.3 10.2 %copy-start.31 = (f32[3584]{0:T(1024)S(1)}, f32[3584]{0:T(1024)}, u32[]{:S(2)}) copy-start(f32[3584]{0:T(1024)} %param.27) | copy-start | bytes 43012
  16.3 10.2 %copy-start.32 = (f32[14]{0:T(128)S(1)}, f32[14]{0:T(128)}, u32[]{:S(2)}) copy-start(f32[14]{0:T(128)} %param.32) | copy-start | bytes 172
  16.3 10.3 %copy-start.33 = (f32[14]{0:T(128)S(1)}, f32[14]{0:T(128)}, u32[]{:S(2)}) copy-start(f32[14]{0:T(128)} %param.33) | copy-start | bytes 172
  16.3 10.5 %copy-start.34 = (f32[14]{0:T(128)S(1)}, f32[14]{0:T(128)}, u32[]{:S(2)}) copy-start(f32[14]{0:T(128)} %param.34) | copy-start | bytes 172
  16.8 41.4 %copy-start.17 = (s32[4]{0:T(128)}, s32[4]{0:T(128)S(1)}, u32[]{:S(2)}) copy-start(s32[4]{0:T(128)S(1)} %pad_add_fusion.idx_ref) | copy-start | bytes 52
  20.8 22.9 %collective-permute-start = (bf16[112,2048]{1,0:T(8,128)(2,1)}, bf16[112,2048]{1,0:T(8,128)(2,1)}, u32[]{:S(2)}, u32[]{:S(2)}) collective-permute-start(bf16[112,2048]{1,0:T(8,128)(2,1)} %get-tuple-element.21), channel_id=1, source_target_pairs={{0,1},{1,0},{2,3},{3,2},{4,5},{5,4},{6,7},{7,6},{8,9},{9,8},{10,11... | collective-permute-start | bytes 1376264 | tf_op jit(solution)/shard_map/ppermute | solution.py:35
  23.8 34.3 %collective-permute-start.1 = (bf16[112,2048]{1,0:T(8,128)(2,1)}, bf16[112,2048]{1,0:T(8,128)(2,1)}, u32[]{:S(2)}, u32[]{:S(2)}) collective-permute-start(bf16[112,2048]{1,0:T(8,128)(2,1)} %get-tuple-element.22), channel_id=1, source_target_pairs={{0,2},{1,3},{2,0},{3,1},{4,6},{5,7},{6,4},{7,5},{8,10},{9,11},{10,... | collective-permute-start | bytes 1376264 | tf_op jit(solution)/shard_map/ppermute | solution.py:35
  26.5 31.7 %collective-permute-start.2 = (bf16[112,2048]{1,0:T(8,128)(2,1)}, bf16[112,2048]{1,0:T(8,128)(2,1)}, u32[]{:S(2)}, u32[]{:S(2)}) collective-permute-start(bf16[112,2048]{1,0:T(8,128)(2,1)} %get-tuple-element.23), channel_id=1, source_target_pairs={{0,3},{1,2},{2,1},{3,0},{4,7},{5,6},{6,5},{7,4},{8,11},{9,10},{10,... | collective-permute-start | bytes 1376264 | tf_op jit(solution)/shard_map/ppermute | solution.py:35
  60.8 63.1 %all-to-all-start = ((bf16[4,224,896]{2,1,0:T(8,128)(2,1)}), bf16[4,224,896]{2,1,0:T(8,128)(2,1)}, u32[]{:S(2)}, u32[]{:S(2)}) async-start(bf16[4,224,896]{2,1,0:T(8,128)(2,1)} %copy-done.11), calls=%async_computation | async-start | bytes 3211264 | tf_op jit(solution)/shard_map/all_to_all | solution.py:104
  72.1 259.1 %all-gather.5.cloned.1.call-start = ((), (), s32[]{:S(2)}) async-start(), calls=%async_computation.2 | async-start | bytes 14450688 | tf_op jit(solution)/shard_map/all_gather | solution.py:170
  72.1 51.9 %collective-permute-start.4 = (bf16[448,2048]{1,0:T(8,128)(2,1)}, bf16[448,2048]{1,0:T(8,128)(2,1)}, u32[]{:S(2)}, u32[]{:S(2)}) collective-permute-start(bf16[448,2048]{1,0:T(8,128)(2,1)} %copy-done.8), channel_id=1, source_target_pairs={{0,8},{4,12},{8,0},{12,4},{16,24},{20,28},{24,16},{28,20},{1,9},{5... | collective-permute-start | bytes 5505032 | tf_op jit(solution)/shard_map/ppermute | solution.py:35
  73.6 50.4 %collective-permute-start.5 = (bf16[448,2048]{1,0:T(8,128)(2,1)}, bf16[448,2048]{1,0:T(8,128)(2,1)}, u32[]{:S(2)}, u32[]{:S(2)}) collective-permute-start(bf16[448,2048]{1,0:T(8,128)(2,1)} %copy-done.8), channel_id=1, source_target_pairs={{0,16},{4,20},{8,24},{12,28},{16,0},{20,4},{24,8},{28,12},{1,17},{... | collective-permute-start | bytes 5505032 | tf_op jit(solution)/shard_map/ppermute | solution.py:35
  81.2 4.5 copy-start.9
  124.0 76.5 %all-to-all-start.1 = ((bf16[4,224,1792]{2,1,0:T(8,128)(2,1)}), bf16[4,224,1792]{2,1,0:T(8,128)(2,1)}, u32[]{:S(2)}, u32[]{:S(2)}) async-start(bf16[4,224,1792]{2,1,0:T(8,128)(2,1)} %copy-done.5), calls=%async_computation.1 | async-start | bytes 6422528 | tf_op jit(solution)/shard_map/all_to_all | solution.py:104
  128.7 215.3 %all-gather.7.cloned.1.call-start = ((), (), s32[]{:S(2)}) async-start(), calls=%async_computation.3 | async-start | bytes 28901376 | tf_op jit(solution)/shard_map/all_gather | solution.py:170
  128.8 44.1 %collective-permute-start.3 = (bf16[448,2048]{1,0:T(8,128)(2,1)S(1)}, bf16[448,2048]{1,0:T(8,128)(2,1)}, u32[]{:S(2)}, u32[]{:S(2)}) collective-permute-start(bf16[448,2048]{1,0:T(8,128)(2,1)S(1)} %copy-done.9), channel_id=1, source_target_pairs={{0,4},{4,0},{8,12},{12,8},{16,20},{20,16},{24,28},{28,24},{1,5},{5... | collective-permute-start | bytes 5505032 | tf_op jit(solution)/shard_map/ppermute | solution.py:35
  128.9 44.0 %collective-permute-start.7 = (bf16[448,2048]{1,0:T(8,128)(2,1)}, bf16[448,2048]{1,0:T(8,128)(2,1)}, u32[]{:S(2)}, u32[]{:S(2)}) collective-permute-start(bf16[448,2048]{1,0:T(8,128)(2,1)} %collective-permute-done.5.refs_3_), channel_id=1, source_target_pairs={{0,4},{4,0},{8,12},{12,8},{16,20},{20,16},{24,28},{28,24},{1,5},{5... | collective-permute-start | bytes 5505032 | tf_op jit(solution)/shard_map/ppermute | solution.py:35
  130.6 42.3 %collective-permute-start.6 = (bf16[448,2048]{1,0:T(8,128)(2,1)}, bf16[448,2048]{1,0:T(8,128)(2,1)}, u32[]{:S(2)}, u32[]{:S(2)}) collective-permute-start(bf16[448,2048]{1,0:T(8,128)(2,1)} %collective-permute-done.4.refs_2_), channel_id=1, source_target_pairs={{0,4},{4,0},{8,12},{12,8},{16,20},{20,16},{24,28},{28,24},{1,5},{5... | collective-permute-start | bytes 5505032 | tf_op jit(solution)/shard_map/ppermute | solution.py:35
  130.7 39.9 %collective-permute-start.8 = (bf16[224,2048]{1,0:T(8,128)(2,1)S(1)}, bf16[224,2048]{1,0:T(8,128)(2,1)S(1)}, u32[]{:S(2)}, u32[]{:S(2)}) collective-permute-start(bf16[224,2048]{1,0:T(8,128)(2,1)S(1)} %slice.26), channel_id=1, source_target_pairs={{0,8},{4,12},{8,0},{12,4},{16,24},{20,28},{24,16},{28,20},{1,9},{5... | collective-permute-start | bytes 2752520 | tf_op jit(solution)/shard_map/ppermute | solution.py:35
  133.6 39.2 %collective-permute-start.9 = (bf16[224,2048]{1,0:T(8,128)(2,1)S(1)}, bf16[224,2048]{1,0:T(8,128)(2,1)}, u32[]{:S(2)}, u32[]{:S(2)}) collective-permute-start(bf16[224,2048]{1,0:T(8,128)(2,1)S(1)} %slice.27), channel_id=1, source_target_pairs={{0,16},{4,20},{8,24},{12,28},{16,0},{20,4},{24,8},{28,12},{1,17},{... | collective-permute-start | bytes 2752520 | tf_op jit(solution)/shard_map/ppermute | solution.py:35
  170.7 2.6 collective-permute-start.10
  172.8 2.8 collective-permute-start.11
  172.8 15.7 %copy-start.20 = (f32[4,128]{1,0:T(4,128)S(1)}, f32[4,128]{1,0:T(4,128)}, u32[]{:S(2)}) copy-start(f32[4,128]{1,0:T(4,128)} %bc_taps_ref.1) | copy-start | bytes 6148
  177.7 10.8 %copy-start.19 = (f32[4,896]{1,0:T(4,128)S(1)}, f32[4,896]{1,0:T(4,128)}, u32[]{:S(2)}) copy-start(f32[4,896]{1,0:T(4,128)} %taps_ref.1) | copy-start | bytes 43012
  194.9 54.6 %copy-start.12 = (bf16[384,896]{1,0:T(8,128)(2,1)}, bf16[384,896]{1,0:T(8,128)(2,1)S(1)}, u32[]{:S(2)}) copy-start(bf16[384,896]{1,0:T(8,128)(2,1)S(1)} %get-tuple-element.32.refs_0_) | copy-start | bytes 2064388
  200.6 30.7 %collective-permute-start.12 = (bf16[384,896]{1,0:T(8,128)(2,1)S(1)}, bf16[384,896]{1,0:T(8,128)(2,1)S(1)}, u32[]{:S(2)}, u32[]{:S(2)}) collective-permute-start(bf16[384,896]{1,0:T(8,128)(2,1)S(1)} %get-tuple-element.32.refs_0_), channel_id=1, source_target_pairs={{0,1},{1,0},{2,3},{3,2},{4,5},{5,4},{6,7},{7,6},{8,9},{9,8},{10,11... | collective-permute-start | bytes 2064392 | tf_op jit(solution)/shard_map/ppermute | solution.py:35
  200.7 48.8 %collective-permute-start.13 = (bf16[384,896]{1,0:T(8,128)(2,1)S(1)}, bf16[384,896]{1,0:T(8,128)(2,1)S(1)}, u32[]{:S(2)}, u32[]{:S(2)}) collective-permute-start(bf16[384,896]{1,0:T(8,128)(2,1)S(1)} %get-tuple-element.32.refs_0_), channel_id=1, source_target_pairs={{0,2},{1,3},{2,0},{3,1},{4,6},{5,7},{6,4},{7,5},{8,10},{9,11},{10,... | collective-permute-start | bytes 2064392 | tf_op jit(solution)/shard_map/ppermute | solution.py:35
  202.7 46.8 %collective-permute-start.14 = (bf16[384,896]{1,0:T(8,128)(2,1)S(1)}, bf16[384,896]{1,0:T(8,128)(2,1)}, u32[]{:S(2)}, u32[]{:S(2)}) collective-permute-start(bf16[384,896]{1,0:T(8,128)(2,1)S(1)} %get-tuple-element.32.refs_0_), channel_id=1, source_target_pairs={{0,3},{1,2},{2,1},{3,0},{4,7},{5,6},{6,5},{7,4},{8,11},{9,10},{10,... | collective-permute-start | bytes 2064392 | tf_op jit(solution)/shard_map/ppermute | solution.py:35
  231.2 18.3 %copy-start.24 = (bf16[384,896]{1,0:T(8,128)(2,1)}, bf16[384,896]{1,0:T(8,128)(2,1)S(1)}, u32[]{:S(2)}) copy-start(bf16[384,896]{1,0:T(8,128)(2,1)S(1)} %collective-permute-done.12.refs_1_) | copy-start | bytes 2064388
  259.9 15.3 %copy-start.22 = (bf16[896,384]{1,0:T(8,128)(2,1)S(1)}, bf16[896,384]{1,0:T(8,128)(2,1)}, u32[]{:S(2)}) copy-start(bf16[896,384]{1,0:T(8,128)(2,1)} %mixer.1.refs_5_) | copy-start | bytes 2064388
  259.9 39.3 %collective-permute-start.15 = (bf16[896,384]{1,0:T(8,128)(2,1)}, bf16[896,384]{1,0:T(8,128)(2,1)S(1)}, u32[]{:S(2)}, u32[]{:S(2)}) collective-permute-start(bf16[896,384]{1,0:T(8,128)(2,1)} %mixer.1.refs_5_), channel_id=1, source_target_pairs={{0,1},{1,0},{2,3},{3,2},{4,5},{5,4},{6,7},{7,6},{8,9},{9,8},{10,11... | collective-permute-start | bytes 2064392 | tf_op jit(solution)/shard_map/ppermute | solution.py:35
  272.6 49.0 %collective-permute-start.16 = (bf16[896,384]{1,0:T(8,128)(2,1)}, bf16[896,384]{1,0:T(8,128)(2,1)S(1)}, u32[]{:S(2)}, u32[]{:S(2)}) collective-permute-start(bf16[896,384]{1,0:T(8,128)(2,1)} %mixer.1.refs_5_), channel_id=1, source_target_pairs={{0,2},{1,3},{2,0},{3,1},{4,6},{5,7},{6,4},{7,5},{8,10},{9,11},{10,... | collective-permute-start | bytes 2064392 | tf_op jit(solution)/shard_map/ppermute | solution.py:35
  272.6 49.1 %collective-permute-start.17 = (bf16[896,384]{1,0:T(8,128)(2,1)}, bf16[896,384]{1,0:T(8,128)(2,1)S(1)}, u32[]{:S(2)}, u32[]{:S(2)}) collective-permute-start(bf16[896,384]{1,0:T(8,128)(2,1)} %mixer.1.refs_5_), channel_id=1, source_target_pairs={{0,3},{1,2},{2,1},{3,0},{4,7},{5,6},{6,5},{7,4},{8,11},{9,10},{10,... | collective-permute-start | bytes 2064392 | tf_op jit(solution)/shard_map/ppermute | solution.py:35
  342.2 18.5 %copy-start.14 = (bf16[384,896]{1,0:T(8,128)(2,1)S(1)}, bf16[384,896]{1,0:T(8,128)(2,1)}, u32[]{:S(2)}) copy-start(bf16[384,896]{1,0:T(8,128)(2,1)} %qkv.2.q_ref) | copy-start | bytes 2064388
  364.4 59.3 %copy-start.13 = (bf16[384,896]{1,0:T(8,128)(2,1)}, bf16[384,896]{1,0:T(8,128)(2,1)S(1)}, u32[]{:S(2)}) copy-start(bf16[384,896]{1,0:T(8,128)(2,1)S(1)} %attend.1.refs_0_) | copy-start | bytes 2064388
  364.4 35.6 %collective-permute-start.18 = (bf16[384,896]{1,0:T(8,128)(2,1)S(1)}, bf16[384,896]{1,0:T(8,128)(2,1)S(1)}, u32[]{:S(2)}, u32[]{:S(2)}) collective-permute-start(bf16[384,896]{1,0:T(8,128)(2,1)S(1)} %attend.1.refs_0_), channel_id=1, source_target_pairs={{0,1},{1,0},{2,3},{3,2},{4,5},{5,4},{6,7},{7,6},{8,9},{9,8},{10,11... | collective-permute-start | bytes 2064392 | tf_op jit(solution)/shard_map/ppermute | solution.py:35
  374.9 48.8 %collective-permute-start.19 = (bf16[384,896]{1,0:T(8,128)(2,1)S(1)}, bf16[384,896]{1,0:T(8,128)(2,1)S(1)}, u32[]{:S(2)}, u32[]{:S(2)}) collective-permute-start(bf16[384,896]{1,0:T(8,128)(2,1)S(1)} %attend.1.refs_0_), channel_id=1, source_target_pairs={{0,2},{1,3},{2,0},{3,1},{4,6},{5,7},{6,4},{7,5},{8,10},{9,11},{10,... | collective-permute-start | bytes 2064392 | tf_op jit(solution)/shard_map/ppermute | solution.py:35
  375.2 48.5 %collective-permute-start.20 = (bf16[384,896]{1,0:T(8,128)(2,1)S(1)}, bf16[384,896]{1,0:T(8,128)(2,1)}, u32[]{:S(2)}, u32[]{:S(2)}) collective-permute-start(bf16[384,896]{1,0:T(8,128)(2,1)S(1)} %attend.1.refs_0_), channel_id=1, source_target_pairs={{0,3},{1,2},{2,1},{3,0},{4,7},{5,6},{6,5},{7,4},{8,11},{9,10},{10,... | collective-permute-start | bytes 2064392 | tf_op jit(solution)/shard_map/ppermute | solution.py:35
  377.3 70.7 %copy-start.28 = (f32[1,14,64,64]{3,2,1,0:T(8,128)S(1)}, f32[1,14,64,64]{3,2,1,0:T(8,128)}, u32[]{:S(2)}) copy-start(f32[1,14,64,64]{3,2,1,0:T(8,128)} %param.26) | copy-start | bytes 688132
  400.0 23.7 %copy-start.25 = (bf16[384,896]{1,0:T(8,128)(2,1)}, bf16[384,896]{1,0:T(8,128)(2,1)S(1)}, u32[]{:S(2)}) copy-start(bf16[384,896]{1,0:T(8,128)(2,1)S(1)} %collective-permute-done.18.refs_1_) | copy-start | bytes 2064388
  424.5 34.7 %copy-start.1 = (bf16[4,128,3,896]{3,1,2,0:T(8,128)(2,1)S(1)}, bf16[4,128,3,896]{3,1,2,0:T(8,128)(2,1)}, u32[]{:S(2)}) copy-start(bf16[4,128,3,896]{3,1,2,0:T(8,128)(2,1)} %param.40) | copy-start | bytes 8257540
  433.9 23.5 %copy-start.18 = (s32[4]{0:T(128)S(1)}, s32[4]{0:T(128)}, u32[]{:S(2)}) copy-start(s32[4]{0:T(128)} %copy-done.17) | copy-start | bytes 52
  435.2 17.0 %collective-permute-start.21 = (bf16[224,384]{1,0:T(8,128)(2,1)S(1)}, bf16[224,384]{1,0:T(8,128)(2,1)S(1)}, u32[]{:S(2)}, u32[]{:S(2)}) collective-permute-start(bf16[224,384]{1,0:T(8,128)(2,1)S(1)} %get-tuple-element.40), channel_id=1, source_target_pairs={{0,1},{1,0},{2,3},{3,2},{4,5},{5,4},{6,7},{7,6},{8,9},{9,8},{10,11... | collective-permute-start | bytes 516104 | tf_op jit(solution)/shard_map/ppermute | solution.py:35
  445.6 11.9 %collective-permute-start.22 = (bf16[224,384]{1,0:T(8,128)(2,1)S(1)}, bf16[224,384]{1,0:T(8,128)(2,1)S(1)}, u32[]{:S(2)}, u32[]{:S(2)}) collective-permute-start(bf16[224,384]{1,0:T(8,128)(2,1)S(1)} %get-tuple-element.39), channel_id=1, source_target_pairs={{0,2},{1,3},{2,0},{3,1},{4,6},{5,7},{6,4},{7,5},{8,10},{9,11},{10,... | collective-permute-start | bytes 516104 | tf_op jit(solution)/shard_map/ppermute | solution.py:35
  445.6 11.9 %collective-permute-start.23 = (bf16[224,384]{1,0:T(8,128)(2,1)S(1)}, bf16[224,384]{1,0:T(8,128)(2,1)S(1)}, u32[]{:S(2)}, u32[]{:S(2)}) collective-permute-start(bf16[224,384]{1,0:T(8,128)(2,1)S(1)} %get-tuple-element.38), channel_id=1, source_target_pairs={{0,3},{1,2},{2,1},{3,0},{4,7},{5,6},{6,5},{7,4},{8,11},{9,10},{10,... | collective-permute-start | bytes 516104 | tf_op jit(solution)/shard_map/ppermute | solution.py:35
  (16 other events, 28.6 us)
Sparse Core Ops, SparseCore 0:
  10.9 86.0 all-gather.8
  124.1 90.3 all-gather.4
  216.4 127.5 all-gather.6
where the time goes:
time: 467 us; the launch traced here: 466 us
  waiting for transfers between devices  254 us (54%)
  Pallas kernels  81.3 us (17%)
  starting transfers between devices  72.9 us (16%)
  local copies, waits for them, and re-layouts  36.9 us (8%)
  between operations  16.1 us (3%)
  other arithmetic  4.81 us (1%)
    ppermute x24, waiting for transfers between devices, exchange(): return lax.ppermute(value, axis, [(i, i ^ bits) for i in range(count)])  246 us
    ppermute x24, starting transfers between devices, exchange(): return lax.ppermute(value, axis, [(i, i ^ bits) for i in range(count)])  56.8 us
    pallas_call x2, Pallas kernels, rows_matmul(): pl.pallas_call(rows_kernel, grid=(owners,), in_specs=[pl.BlockSpec((1, to...  27.7 us
    unnamed x72, local copies, waits for them, and re-layouts  21.5 us
    pallas_call x2, Pallas kernels, columns(): pl.pallas_call(partial(columns_kernel, len(parts), ordered, scaled), grid...  18.9 us
    all_to_all x2, starting transfers between devices, tp_trade(): out = lax.all_to_all(slices, 'tp', split_axis=0, concat_axis=0, tiled=True)  16 us
    pallas_call x1, Pallas kernels, pieces_matmul(): pl.pallas_call(partial(pieces_kernel, places), in_specs=[pl.BlockSpec(mem...  10.8 us
  transfers between devices with their start and end apart: 29, of which 17 were waited for; matrix products, arithmetic and copies ran while one was open for 4% of the time, Pallas kernels for 11%

commit v1 on v0

--- a/solution.py
+++ b/solution.py
@@ -130,6 +130,31 @@
 
 def tp_send(pieces):
     return [pieces[0]] + [exchange(p, "tp", b) for b, p in enumerate(pieces) if b]
+
+
+def tp_step(pair):
+    count = lax.axis_size("tp")
+    return (
+        lax.ppermute(pair[0], "tp", [(i, i + 1) for i in range(count - 1)]),
+        lax.ppermute(pair[1], "tp", [(i + 1, i) for i in range(count - 1)]),
+    )
+
+
+def tp_line(own):
+    pairs = [(own, own)]
+    for _ in range(lax.axis_size("tp") - 1):
+        pairs.append(tp_step(pairs[-1]))
+    return pairs
+
+
+def tp_stack(pairs, tp_index):
+    count = len(pairs)
+    out = jnp.zeros((count,) + pairs[0][0].shape, pairs[0][0].dtype)
+    out = lax.dynamic_update_index_in_dim(out, pairs[0][0], tp_index, 0)
+    for j in range(1, count):
+        piece = jnp.where(tp_index >= j, pairs[j][0], pairs[count - j][1])
+        out = lax.dynamic_update_index_in_dim(out, piece, (tp_index - j) % count, 0)
+    return out
 
 
 def by_xor(slices):
@@ -178,6 +203,7 @@
 
     def first(self):
         own = self.own
+        self.core = exchange(own, "req", 1)
         if self.count == 8:
             self.px, self.py = exchange(own, "req", 2), exchange(own, "req", 4)
             return [self.px, self.py]
@@ -192,13 +218,14 @@
     def second(self):
         if self.count != 8:
             self.pieces = [(at, 0, v) for at, v in self.moved]
-            self.pieces += [(at ^ 1, 0, exchange(v, "req", 1)) for at, v in self.moved]
+            self.pieces += [(at ^ 1, 0, exchange(v, "req", 1)) for at, v in self.moved[1:]]
+            self.pieces.append((1, 0, self.core))
             return []
         half = -(-self.own.shape[0] // 32) * 16
         self.half = half
         self.d0 = exchange(self.py[:half], "req", 2)
         self.d1 = exchange(self.px[half:], "req", 4)
-        self.pieces.append((1, 0, exchange(self.own, "req", 1)))
+        self.pieces.append((1, 0, self.core))
         self.pieces += [(2, 0, self.px), (4, 0, self.py)]
         self.pieces += [(3, 0, exchange(self.px, "req", 1)), (5, 0, exchange(self.py, "req", 1))]
         return [self.d0, self.d1]
@@ -435,70 +462,117 @@
     )(info, zx, taps, bc_taps, *per_head)
 
 
-def column_weights(gathered, which):
-    owners, _, rows, width = gathered.shape
-    if rows % 16:
-        gathered = gathered[:, which].reshape(1, 1, owners * rows, width)
-        which = 0
-    block = (gathered.shape[0], 1) + gathered.shape[2:]
-    return gathered, pl.BlockSpec(block, lambda i, x: (0, which, 0, 0))
-
-
-def columns_kernel(tp_count, ordered, scaled, idx_ref, *refs):
-    a_refs, gain_ref, stream_ref, w_ref, out_ref = refs[:tp_count], *refs[tp_count:]
-    tp = 0 if ordered else idx_ref[1]
-    tokens, share = a_refs[0].shape
-    rows = out_ref.shape[0]
-    squares = jnp.zeros((tokens, 1), F32)
-    total = None
-    for b in range(tp_count):
-        act = a_refs[b][...]
+def columns_part(scaled, steps, idx_ref, refs):
+    each = 3 if scaled else 2
+    squares = total = None
+    for i, step in enumerate(steps):
+        act_ref, w_ref = refs[each * i], refs[each * i + 1]
+        act = act_ref[...]
         if scaled:
             raw = act.astype(F32)
-            squares = squares + jnp.sum(raw * raw, axis=1, keepdims=True)
-            act = (raw * gain_ref[tp ^ b]).astype(BF)
-        if ordered:
-            weights = w_ref[:, 0, :, b * share : (b + 1) * share]
-        else:
-            weights = w_ref[:, 0, :, pl.ds(pl.multiple_of((tp ^ b) * share, 128), share)]
-        part = dot(weights.reshape(rows, share), act, NT)
+            square = jnp.sum(raw * raw, axis=1, keepdims=True)
+            squares = square if squares is None else squares + square
+            act = (raw * refs[each * i + 2][0]).astype(BF)
+        part = dot(w_ref[...], act, NT)
         total = part if total is None else total + part
+    return total, squares
+
+
+def columns_kernel(scaled, steps, begin, last, denominator, idx_ref, *refs):
+    count = (3 if scaled else 2) * len(steps)
+    total, squares = columns_part(scaled, steps, idx_ref, refs)
+    rest = list(refs[count:])
+    if not begin:
+        total = total + rest.pop(0)[...]
+        if scaled:
+            squares = squares + rest.pop(0)[...]
+    if not last:
+        rest[0][...] = total
+        if scaled:
+            rest[1][...] = jnp.broadcast_to(squares, rest[1].shape)
+        return
+    stream_ref, out_ref = rest
     if scaled:
-        scale = lax.rsqrt(squares / (share * tp_count) + EPSILON)
-        total = total * jnp.broadcast_to(scale, (tokens, 128)).T[0:1, :]
-        out_ref[...] = (stream_ref[...].astype(F32) + total).astype(BF)
-    else:
-        total = stream_ref[...].astype(F32) + total
+        scale = lax.rsqrt(squares / denominator + EPSILON)
+        total = total * scale.T[0:1, :]
+    total = stream_ref[...].astype(F32) + total
+    if not scaled:
         place = lax.broadcasted_iota(jnp.int32, total.shape, 1)
         keep = place < jnp.where(idx_ref[3] > 0, idx_ref[2], 0)
-        out_ref[...] = jnp.where(keep, total, 0.0).astype(BF)
-
-
-def columns(gathered, which, idx, parts, gain, stream, scaled):
-    ordered = parts[0].shape[1] % 128 != 0
-    if ordered:
-        stacked = jnp.stack(parts)
-        for b, part in enumerate(parts):
-            stacked = lax.dynamic_update_index_in_dim(stacked, part, idx[1] ^ b, 0)
-        parts = [stacked[i] for i in range(len(parts))]
-    weights, spec = column_weights(gathered, which)
+        total = jnp.where(keep, total, 0.0)
+    out_ref[...] = total.astype(BF)
+
+
+def columns_whole(weights, idx, pairs, gain, stream, scaled):
+    acts = tp_stack(pairs, idx[1])
+    count, tokens, share = acts.shape
+    raw = acts.astype(F32)
+    if scaled:
+        acts = (raw * gain).astype(BF)
+    flat = acts.transpose(1, 0, 2).reshape(tokens, count * share)
+    total = dot(weights, flat, NT)
+    if scaled:
+        squares = jnp.sum(raw * raw, axis=(0, 2)) / (count * share)
+        total = total * lax.rsqrt(squares + EPSILON)[None, :]
+    total = stream.astype(F32) + total
+    if not scaled:
+        total = jnp.where(jnp.arange(tokens)[None, :] < idx[2] * (idx[3] > 0), total, 0.0)
+    return total.astype(BF)
+
+
+def columns(weights, idx, own, beside, gain, stream, scaled):
+    tokens, share = own.shape
+    if share % 128:
+        return columns_whole(weights, idx, tp_line(own), gain, stream, scaled)
+    count = lax.axis_size("tp")
+    pairs = [(own, own), tuple(beside)]
 
     def full(v):
-        return pl.BlockSpec(v.shape, lambda i, x: (0,) * v.ndim)
-
-    return pl.pallas_call(
-        partial(columns_kernel, len(parts), ordered, scaled),
-        grid_spec=pltpu.PrefetchScalarGridSpec(
-            num_scalar_prefetch=1,
-            grid=(1,),
-            in_specs=[full(v) for v in parts] + [full(gain), full(stream), spec],
-            out_specs=full(stream),
-        ),
-        out_shape=jax.ShapeDtypeStruct(stream.shape, BF),
-        compiler_params=params(58),
-        cost_estimate=cost(2 * 896 * 384 * 3584, 12 * MB),
-        name="mixer" if scaled else "output",
-    )(idx, *parts, gain, stream, weights)
+        return pl.BlockSpec(v.shape, lambda i, x: (0,) * len(v.shape))
+
+    def run(steps, begun, last):
+        specs, arrays = [], []
+        for step in steps:
+
+            def owner(x, step=step):
+                return jnp.clip(x[1] - step, 0, count - 1)
+
+            specs.append(pl.BlockSpec((tokens, share), lambda i, x: (0, 0)))
+            specs.append(pl.BlockSpec((weights.shape[0], share), lambda i, x, o=owner: (0, o(x))))
+            arrays += [pairs[abs(step)][step < 0], weights]
+            if scaled:
+                specs.append(pl.BlockSpec((1, 1, share), lambda i, x, o=owner: (o(x), 0, 0)))
+                arrays.append(gain)
+        more = list(begun) + ([stream] if last else [])
+        if last:
+            outs = [jax.ShapeDtypeStruct(stream.shape, BF)]
+        else:
+            outs = [jax.ShapeDtypeStruct(stream.shape, F32)]
+            if scaled:
+                outs.append(jax.ShapeDtypeStruct((tokens, 128), F32))
+        return pl.pallas_call(
+            partial(columns_kernel, scaled, steps, not begun, last, share * count),
+            grid_spec=pltpu.PrefetchScalarGridSpec(
+                num_scalar_prefetch=1,
+                grid=(1,),
+                in_specs=specs + [full(v) for v in more],
+                out_specs=tuple(full(v) for v in outs),
+            ),
+            out_shape=tuple(outs),
+            compiler_params=params(50),
+            cost_estimate=cost(len(steps) * 2 * 896 * 384 * 896, len(steps) * 3 * MB),
+            name=("far" if last else "middle" if begun else "near") + ("_mixer" if scaled else "_output"),
+        )(idx, *arrays, *more)
+
+    steps, begun = [0, 1, -1], []
+    for j in range(2, count):
+        ahead = tp_step(pairs[-1])
+        begun = run(steps, begun, False)
+        *ahead, first = after(list(ahead) + [begun[0]], [])
+        begun = [first] + list(begun[1:])
+        pairs.append(tuple(ahead))
+        steps = [j, -j]
+    return run(steps, begun, True)[0]
 
 
 def join_kernel(which_ref, mid_ref, embeds_ref, gain_ref, down_ref, act_ref, low_ref):
@@ -671,8 +745,7 @@
     small = jnp.pad(small, ((0, 0), (0, 256 - small.shape[1])))
     zx_send = prepare_input(idx, trainer_gate_input_weight.transpose(1, 0, 2), small, tp_count)
     zx_received = tp_send(zx_send)
-    o_pair = jnp.stack([trainer_mamba_output_weight.astype(BF).T, trainer_output_weight.astype(BF).T])
-    o_pair = gather_rows(o_pair[None])
+    out_server = gather_rows(trainer_mamba_output_weight.astype(BF).T)
     q_send, kv_send = prepare(
         trainer_query_key_value_weight.transpose(1, 0, 2), tp_count, [(0,), (1, 2)]
     )
@@ -680,25 +753,32 @@
     per_head = head_rows(step_bias, head_decay_rate, direct_head_term, heads, inner)
     zx_own = tp_place(idx, zx_received)
 
-    zx_own, q_send, *_ = after([zx_own, q_send], [normed_in] + per_head)
-    zx_gather = Gather(zx_own)
-    zx_first = zx_gather.first()
-    q_own = tp_trade(q_send)
     stream_t = hidden[0].T.reshape(req_count, tp_count, rows, seq_len)
     stream_t = lax.dynamic_index_in_dim(stream_t, tp_index, 1, keepdims=False)
     stream_t = stream_t.reshape(req_count * rows, seq_len)
     ups = lax.dynamic_index_in_dim(adapter_up_maps, adapter[0], 0, keepdims=False)
     ups = [ups[:, 0], ups[:, 1:].reshape(ups.shape[0], -1)]
+    o_own = trainer_output_weight.astype(BF).T
+
+    early = [normed_in, q_send, kv_send, stream_t, o_own] + ups + per_head
+    zx_own, *early = after([zx_own] + early, [])
+    normed_in, q_send, kv_send, stream_t, o_own = early[:5]
+    ups, per_head = early[5:7], early[7:]
+    zx_gather = Gather(zx_own)
+    zx_first = zx_gather.first()
+    q_send, zx_gather.core = after([q_send, zx_gather.core], [])
+    q_own = tp_trade(q_send)
     gain_all = zx_own.reshape(tp_count, rows, -1)[:, :, 2 * inner + used :].astype(F32)
     gain_all = (gain_all[:, :, :each] + gain_all[:, :, each : 2 * each]).reshape(tp_count, 1, inner)
 
-    held = after(zx_first + [kv_send, q_own], [stream_t, gain_all] + ups)
+    held = after(zx_first + [kv_send, q_own], [gain_all])
     if req_count == 8:
         zx_gather.refresh(["px", "py"], held[:2])
     kv_send, q_own = held[-2:]
+    kv_own = tp_trade(kv_send)
+    zx_second = zx_gather.second()
+    q_own, *_ = after([q_own], [out_server])
     q_server = gather_rows(q_own)
-    zx_second = zx_gather.second()
-    kv_own = tp_trade(kv_send)
     zx_gather.third()
 
     zx = pieces_matmul(normed_in, zx_gather)
@@ -706,21 +786,20 @@
     raw, final = run_scan(
         zx, info, convolution_inner_taps, convolution_bc_taps, per_head, heads, inner, state_dim
     )
-    raw, kv_own = after([raw, kv_own], [])
+    beside = tp_step((raw, raw))
+    kv_own, *beside = after([kv_own, *beside], [])
     kv_server = gather_rows(kv_own)
-    raws = tp_send([raw] * tp_count)
-    mid_own = columns(o_pair, 0, idx, raws, gain_all, stream_t, True)
-    mids = jnp.zeros((tp_count,) + mid_own.shape, BF)
-    for b, moved in enumerate(tp_send([mid_own] * tp_count)):
-        mids = lax.dynamic_update_index_in_dim(mids, moved, tp_index ^ b, 0)
-    mid = mids.reshape(tp_count, req_count, rows, seq_len).transpose(1, 0, 2, 3)
+    mid_own = columns(out_server, idx, raw, beside, gain_all, stream_t, True)
+    mid = tp_stack(tp_line(mid_own), tp_index)
+    mid = mid.reshape(tp_count, req_count, rows, seq_len).transpose(1, 0, 2, 3)
     mid = mid.reshape(width, seq_len)
     act, low = join(mid, embeds[0], attention_norm_gain[None, :], adapter_down_maps, adapter, 4)
     queries = rows_matmul(act, q_server, low, ups[0])
+    o_own, kv_server = after([o_own, kv_server], [queries])
+    o_server = gather_rows(o_own)
     keys_values = rows_matmul(act, kv_server, low, ups[1])
     attended = attend(queries, keys_values, lengths, queries.shape[1] // HS)
-    whole = tp_send([attended] * tp_count)
-    result = columns(o_pair, 1, idx, whole, gain_all, mid_own, False)
+    result = columns(o_server, idx, attended, tp_step((attended, attended)), gain_all, mid_own, False)
     result = tp_send(by_xor(result.reshape(tp_count, -1, seq_len)))
     result = finish(idx, result, rows)
     final = final.reshape((1, heads, inner // heads, state_dim))

time: 467 us -> 453 us (0.970)
  waiting for transfers between devices: 254 us -> 207 us
  Pallas kernels: 81.3 us -> 98.7 us
  starting transfers between devices: 72.9 us -> 82.3 us
    ppermute x24 -> x15, waiting for transfers between devices: 246 us -> 100 us  [exchange(): return lax.ppermute(value, axis, [(i, i ^ bits) for i in range(count)])]
    ppermute x0 -> x18, waiting for transfers between devices: none -> 93.3 us  [the longest x9 50.9 us: tp_step(): lax.ppermute(pair[1], 'tp', [(i + 1, i) for i in range(count - 1)])]
    ppermute x0 -> x18, starting transfers between devices: none -> 49.8 us  [the longest x9 37.8 us: tp_step(): lax.ppermute(pair[0], 'tp', [(i, i + 1) for i in range(count - 1)])]
    ppermute x24 -> x15, starting transfers between devices: 56.8 us -> 15.8 us  [exchange(): return lax.ppermute(value, axis, [(i, i ^ bits) for i in range(count)])]
    pallas_call x2 -> x6, Pallas kernels: 18.9 us -> 34.1 us  [run(): pl.pallas_call(partial(columns_kernel, scaled, steps, not begun, last, sh...]
    all_gather x3 -> x4, waiting for transfers between devices: 1.81 us -> 13.5 us  [gather_rows(): return lax.all_gather(piece, 'req', axis=0, tiled=True)]
    all_to_all x2, waiting for transfers between devices: 5.62 us -> 0.01 us  [tp_trade(): out = lax.all_to_all(slices, 'tp', split_axis=0, concat_axis=0, tiled=True)]
    transpose x0 -> x2, other arithmetic: none -> 5.08 us  [the longest x1 2.54 us: local(): out_server = gather_rows(trainer_mamba_output_weight.astype(BF).T)]
  transfers between devices with their start and end apart: 29 -> 39, of which waited for: 17 -> 26; matrix products, arithmetic and copies ran while one was open for 4% -> 5% of each run, Pallas kernels for 11% -> 20%
where the time goes in v1:
time: 453 us; the launch traced here: 447 us
  waiting for transfers between devices  207 us (46%)
  Pallas kernels  98.7 us (22%)
  starting transfers between devices  82.3 us (18%)
  local copies, waits for them, and re-layouts  34.5 us (8%)
  between operations  16.7 us (4%)
  other arithmetic  8.15 us (2%)
    ppermute x15, waiting for transfers between devices, exchange(): return lax.ppermute(value, axis, [(i, i ^ bits) for i in range(count)])  100 us
    ppermute x9, waiting for transfers between devices, tp_step(): lax.ppermute(pair[1], 'tp', [(i + 1, i) for i in range(count - 1)])  50.9 us
    ppermute x9, waiting for transfers between devices, tp_step(): lax.ppermute(pair[0], 'tp', [(i, i + 1) for i in range(count - 1)])  42.3 us
    ppermute x9, starting transfers between devices, tp_step(): lax.ppermute(pair[0], 'tp', [(i, i + 1) for i in range(count - 1)])  37.8 us
    pallas_call x6, Pallas kernels, run(): pl.pallas_call(partial(columns_kernel, scaled, steps, not begun, last, sh...  34.1 us
    pallas_call x2, Pallas kernels, rows_matmul(): pl.pallas_call(rows_kernel, grid=(owners,), in_specs=[pl.BlockSpec((1, to...  28.3 us
    unnamed x62, local copies, waits for them, and re-layouts  21.5 us
    all_to_all x2, starting transfers between devices, tp_trade(): out = lax.all_to_all(slices, 'tp', split_axis=0, concat_axis=0, tiled=True)  16.1 us
  transfers between devices with their start and end apart: 39, of which 26 were waited for; matrix products, arithmetic and copies ran while one was open for 5% of the time, Pallas kernels for 20%

profile of v1, /device:TPU:0, one launch (start us, length us, event | category | flops | bytes accessed | tf_op | source)
XLA Modules:
  0.0 447.1 jit_solution(14339735578075825151)
XLA Ops:
  7.2 2.5 convert_bitcast_fusion
  16.2 3.0 collective-permute-start
  19.3 2.6 collective-permute-start.1
  27.8 2.8 copy.45
  32.8 3.7 copy-done.3
  36.6 2.7 prepare.1
  44.1 9.4 %collective-permute-done.1.refs_2_ = bf16[112,2048]{1,0:T(8,128)(2,1)} collective-permute-done((bf16[112,2048]{1,0:T(8,128)(2,1)}, bf16[112,2048]{1,0:T(8,128)(2,1)}, u32[]{:S(2)}, u32[]{:S(2)}) %collective-permute-start.1) | collective-permute-done | bytes 458784 | tf_op jit(solution)/shard_map/ppermute | solution.py:35
  55.1 3.8 collective-permute-done.5.refs_1_
  60.2 11.2 %all-to-all-start = ((bf16[4,224,896]{2,1,0:T(8,128)(2,1)}), bf16[4,224,896]{2,1,0:T(8,128)(2,1)}, u32[]{:S(2)}, u32[]{:S(2)}) async-start(bf16[4,224,896]{2,1,0:T(8,128)(2,1)} %copy-done.8), calls=%async_computation | async-start | bytes 3211264 | tf_op jit(solution)/shard_map/all_to_all | solution.py:104
  74.8 38.5 %collective-permute-done.3.refs_2_ = bf16[448,2048]{1,0:T(8,128)(2,1)} collective-permute-done((bf16[448,2048]{1,0:T(8,128)(2,1)S(1)}, bf16[448,2048]{1,0:T(8,128)(2,1)}, u32[]{:S(2)}, u32[]{:S(2)}) %collective-permute-start.3) | collective-permute-done | bytes 1835040 | tf_op jit(solution)/shard_map/ppermute | solution.py:35
  114.6 4.9 %all-to-all-start.1 = ((bf16[4,224,1792]{2,1,0:T(8,128)(2,1)}), bf16[4,224,1792]{2,1,0:T(8,128)(2,1)}, u32[]{:S(2)}, u32[]{:S(2)}) async-start(bf16[4,224,1792]{2,1,0:T(8,128)(2,1)} %get-tuple-element.63), calls=%async_computation.1 | async-start | bytes 6422528 | tf_op jit(solution)/shard_map/all_to_all | solution.py:104
  125.2 34.2 %collective-permute-done.8.refs_6_ = bf16[224,2048]{1,0:T(8,128)(2,1)} collective-permute-done((bf16[224,2048]{1,0:T(8,128)(2,1)S(1)}, bf16[224,2048]{1,0:T(8,128)(2,1)}, u32[]{:S(2)}, u32[]{:S(2)}) %collective-permute-start.8) | collective-permute-done | bytes 917536 | tf_op jit(solution)/shard_map/ppermute | solution.py:35
  165.4 11.2 %zx.1.zx_ref = bf16[384,2048]{1,0:T(8,128)(2,1)S(1)} custom-call(s32[1]{0:T(128)} %bitcast.req_ref, bf16[8,384,448]{2,1,0:T(8,128)(2,1)} %copy-done.6, bf16[448,2048]{1,0:T(8,128)(2,1)S(1)} %place.1.refs_0_, bf16[448,2048]{1,0:T(8,128)(2,1)S(1)} %copy-done.19, bf16[448,2048]{1,0:T(8,128)(2,1)} %collective-permute-done.3.refs_2_, ...), custom_call_target="tpu_custom_call" | custom-call | flops 5637144576 | bytes 14680064 | tf_op jit(solution)/shard_map/zx/pallas_call | solution.py:287
  176.7 6.4 %scan.1 = (bf16[384,896]{1,0:T(8,128)(2,1)S(1)}, f32[896,64]{1,0:T(8,128)S(1)}) custom-call(s32[2]{0:T(128)S(1)} %pad_add_fusion.1.info_ref, bf16[384,2048]{1,0:T(8,128)(2,1)S(1)} %zx.1.zx_ref, f32[4,896]{1,0:T(4,128)S(1)} %copy-done.20, f32[4,128]{1,0:T(4,128)S(1)} %copy-done.21, f32[1,128]{1,0:T(1,128)S(1)} %pad.19.bias_ref, f32[16,1]{1,0:T(8,128)S(1)} %pad.20.bias_t_ref, ...), custom_call_target="tpu_custom_call" | custom-call | flops 6000000000 | bytes 4194304 | tf_op jit(solution)/shard_map/scan/pallas_call | solution.py:445
  183.9 5.0 %collective-permute-start.12 = (bf16[384,896]{1,0:T(8,128)(2,1)S(1)}, bf16[384,896]{1,0:T(8,128)(2,1)S(1)}, u32[]{:S(2)}, u32[]{:S(2)}) collective-permute-start(bf16[384,896]{1,0:T(8,128)(2,1)S(1)} %get-tuple-element.73.refs_0_), channel_id=1, source_target_pairs={{0,1},{1,2},{2,3},{4,5},{5,6},{6,7},{8,9},{9,10},{10,11},{12,13},{... | collective-permute-start | bytes 2064392 | tf_op jit(solution)/shard_map/ppermute | solution.py:138
  190.2 13.6 %collective-permute-done.12.refs_3_ = bf16[384,896]{1,0:T(8,128)(2,1)S(1)} collective-permute-done((bf16[384,896]{1,0:T(8,128)(2,1)S(1)}, bf16[384,896]{1,0:T(8,128)(2,1)S(1)}, u32[]{:S(2)}, u32[]{:S(2)}) %collective-permute-start.12) | collective-permute-done | bytes 688160 | tf_op jit(solution)/shard_map/ppermute | solution.py:138
  203.8 4.3 collective-permute-done.13.refs_6_
  208.1 3.5 collective-permute-start.14
  213.1 7.3 %near_mixer.1 = (f32[896,384]{1,0:T(8,128)S(1)}, f32[384,128]{1,0:T(8,128)S(1)}) custom-call(s32[4]{0:T(128)S(1)} %pad_add_fusion.idx_ref, bf16[384,896]{1,0:T(8,128)(2,1)S(1)} %get-tuple-element.73.refs_0_, bf16[896,3584]{1,0:T(8,128)(2,1)} %all-gather.5.cloned.1.call-done.refs_1_.refs_4_.refs_7_, f32[4,1,896]{2,1,0:T(1,128)S(1)} %copy.49.refs_2_.refs_5_.refs_8_, ...), custom_call_target="tpu_custom_call" | custom-call | flops 1849688064 | bytes 9437184 | tf_op jit(solution)/shard_map/near_mixer/pallas_call | solution.py:553
  221.5 3.9 collective-permute-done.14.refs_0_
  225.4 4.4 collective-permute-done.15.refs_3_
  233.5 4.9 %middle_mixer.1 = (f32[896,384]{1,0:T(8,128)S(1)}, f32[384,128]{1,0:T(8,128)S(1)}) custom-call(s32[4]{0:T(128)S(1)} %pad_add_fusion.idx_ref, bf16[384,896]{1,0:T(8,128)(2,1)S(1)} %collective-permute-done.14.refs_0_, bf16[896,3584]{1,0:T(8,128)(2,1)} %all-gather.5.cloned.1.call-done.refs_1_.refs_4_.refs_7_, f32[4,1,896]{2,1,0:T(1,128)S(1)} %copy.49.refs_2_.refs_5_.refs_8_, ...), custom_call_target="tpu_custom_call" | custom-call | flops 1233125376 | bytes 6291456 | tf_op jit(solution)/shard_map/middle_mixer/pallas_call | solution.py:553
  239.5 5.6 %collective-permute-done.16.refs_0_ = bf16[384,896]{1,0:T(8,128)(2,1)S(1)} collective-permute-done((bf16[384,896]{1,0:T(8,128)(2,1)S(1)}, bf16[384,896]{1,0:T(8,128)(2,1)S(1)}, u32[]{:S(2)}, u32[]{:S(2)}) %collective-permute-start.16) | collective-permute-done | bytes 688160 | tf_op jit(solution)/shard_map/ppermute | solution.py:138
  245.2 4.2 collective-permute-done.17.refs_3_
  249.3 4.9 %far_mixer.1.refs_5_ = bf16[896,384]{1,0:T(8,128)(2,1)S(1)} custom-call(s32[4]{0:T(128)S(1)} %pad_add_fusion.idx_ref, bf16[384,896]{1,0:T(8,128)(2,1)S(1)} %collective-permute-done.16.refs_0_, bf16[896,3584]{1,0:T(8,128)(2,1)} %all-gather.5.cloned.1.call-done.refs_1_.refs_4_.refs_7_, f32[4,1,896]{2,1,0:T(1,128)S(1)} %copy.49.refs_2_.refs_5_.refs_8_, ...), custom_call_target="tpu_custom_call" | custom-call | flops 1233125376 | bytes 6291456 | tf_op jit(solution)/shard_map/far_mixer/pallas_call | solution.py:553
  255.6 4.6 %collective-permute-start.18 = (bf16[896,384]{1,0:T(8,128)(2,1)S(1)}, bf16[896,384]{1,0:T(8,128)(2,1)S(1)}, u32[]{:S(2)}, u32[]{:S(2)}) collective-permute-start(bf16[896,384]{1,0:T(8,128)(2,1)S(1)} %far_mixer.1.refs_5_), channel_id=1, source_target_pairs={{0,1},{1,2},{2,3},{4,5},{5,6},{6,7},{8,9},{9,10},{10,11},{12,13},{... | collective-permute-start | bytes 2064392 | tf_op jit(solution)/shard_map/ppermute | solution.py:138
  260.2 10.4 %collective-permute-done.19 = bf16[896,384]{1,0:T(8,128)(2,1)S(1)} collective-permute-done((bf16[896,384]{1,0:T(8,128)(2,1)S(1)}, bf16[896,384]{1,0:T(8,128)(2,1)S(1)}, u32[]{:S(2)}, u32[]{:S(2)}) %collective-permute-start.19) | collective-permute-done | bytes 688160 | tf_op jit(solution)/shard_map/ppermute | solution.py:139
  271.8 4.6 %collective-permute-start.22 = (bf16[896,384]{1,0:T(8,128)(2,1)S(1)}, bf16[896,384]{1,0:T(8,128)(2,1)S(1)}, u32[]{:S(2)}, u32[]{:S(2)}) collective-permute-start(bf16[896,384]{1,0:T(8,128)(2,1)S(1)} %collective-permute-done.18), channel_id=1, source_target_pairs={{0,1},{1,2},{2,3},{4,5},{5,6},{6,7},{8,9},{9,10},{10,11},{12,13},{... | collective-permute-start | bytes 2064392 | tf_op jit(solution)/shard_map/ppermute | solution.py:138
  276.4 9.6 %collective-permute-done.20 = bf16[896,384]{1,0:T(8,128)(2,1)S(1)} collective-permute-done((bf16[896,384]{1,0:T(8,128)(2,1)S(1)}, bf16[896,384]{1,0:T(8,128)(2,1)S(1)}, u32[]{:S(2)}, u32[]{:S(2)}) %collective-permute-start.20) | collective-permute-done | bytes 688160 | tf_op jit(solution)/shard_map/ppermute | solution.py:139
  287.4 4.8 %collective-permute-start.23 = (bf16[896,384]{1,0:T(8,128)(2,1)S(1)}, bf16[896,384]{1,0:T(8,128)(2,1)S(1)}, u32[]{:S(2)}, u32[]{:S(2)}) collective-permute-start(bf16[896,384]{1,0:T(8,128)(2,1)S(1)} %collective-permute-done.22), channel_id=1, source_target_pairs={{0,1},{1,2},{2,3},{4,5},{5,6},{6,7},{8,9},{9,10},{10,11},{12,13},{... | collective-permute-start | bytes 2064392 | tf_op jit(solution)/shard_map/ppermute | solution.py:138
  292.6 8.3 %collective-permute-done.21 = bf16[896,384]{1,0:T(8,128)(2,1)} collective-permute-done((bf16[896,384]{1,0:T(8,128)(2,1)S(1)}, bf16[896,384]{1,0:T(8,128)(2,1)}, u32[]{:S(2)}, u32[]{:S(2)}) %collective-permute-start.21) | collective-permute-done | bytes 688160 | tf_op jit(solution)/shard_map/ppermute | solution.py:139
  304.4 6.9 %join.1 = (bf16[4,384,1792]{2,1,0:T(8,128)(2,1)}, bf16[384,128]{1,0:T(8,128)(2,1)S(1)}) custom-call(s32[1]{0:T(128)} %copy.66.which_ref, bf16[3584,384]{1,0:T(8,128)(2,1)S(1)} %bitcast.63, bf16[384,3584]{1,0:T(8,128)(2,1)S(1)} %bitcast.67, f32[1,7168]{1,0:T(1,128)S(1)} %bitcast.70, bf16[4,7168,128]{2,1,0:T(8,128)(2,1)} %down_ref.1), custom_call_target="tpu_custom_call" | custom-call | flops 704643072 | bytes 13631488 | tf_op jit(solution)/shard_map/join/pallas_call | solution.py:603
  311.9 11.0 %qkv.2.q_ref = bf16[384,896]{1,0:T(8,128)(2,1)} custom-call(bf16[4,384,1792]{2,1,0:T(8,128)(2,1)} %get-tuple-element.87.act_ref, bf16[7168,896]{1,0:T(8,128)(2,1)} %all-gather.7.cloned.1.call-done.w_ref, bf16[384,128]{1,0:T(8,128)(2,1)} %copy-done.16, bf16[128,896]{1,0:T(8,128)(2,1)} %slice_bitcast_fusion.1.up_ref), custom_call_target="tpu_custom_call" | custom-call | flops 4932501504 | bytes 12845056 | tf_op jit(solution)/shard_map/qkv/pallas_call | solution.py:324
  323.0 11.9 %all-gather.9.cloned.1.call-done.w_ref = bf16[7168,1792]{1,0:T(8,128)(2,1)} async-done(((bf16[896,1792]{1,0:T(8,128)(2,1)}), bf16[7168,1792]{1,0:T(8,128)(2,1)}) %all-gather.9.cloned.1.call-update) | async-done | bytes 25690128 | tf_op jit(solution)/shard_map/all_gather | solution.py:195
  334.9 17.2 %qkv.3.kv_ref = bf16[384,1792]{1,0:T(8,128)(2,1)} custom-call(bf16[4,384,1792]{2,1,0:T(8,128)(2,1)} %get-tuple-element.87.act_ref, bf16[7168,1792]{1,0:T(8,128)(2,1)} %all-gather.9.cloned.1.call-done.w_ref, bf16[384,128]{1,0:T(8,128)(2,1)} %copy-done.16, bf16[128,1792]{1,0:T(8,128)(2,1)} %bitcast.74), custom_call_target="tpu_custom_call" | custom-call | flops 9865003008 | bytes 25690112 | tf_op jit(solution)/shard_map/qkv/pallas_call | solution.py:324
  355.9 4.2 collective-permute-start.24
  362.2 12.1 %collective-permute-done.24.refs_2_ = bf16[384,896]{1,0:T(8,128)(2,1)} collective-permute-done((bf16[384,896]{1,0:T(8,128)(2,1)S(1)}, bf16[384,896]{1,0:T(8,128)(2,1)}, u32[]{:S(2)}, u32[]{:S(2)}) %collective-permute-start.24) | collective-permute-done | bytes 688160 | tf_op jit(solution)/shard_map/ppermute | solution.py:138
  374.3 5.3 %collective-permute-start.25 = (bf16[384,896]{1,0:T(8,128)(2,1)}, bf16[384,896]{1,0:T(8,128)(2,1)}, u32[]{:S(2)}, u32[]{:S(2)}) collective-permute-start(bf16[384,896]{1,0:T(8,128)(2,1)} %collective-permute-done.24.refs_2_), channel_id=1, source_target_pairs={{0,1},{1,2},{2,3},{4,5},{5,6},{6,7},{8,9},{9,10},{10,11},{12,13},{... | collective-permute-start | bytes 2064392 | tf_op jit(solution)/shard_map/ppermute | solution.py:138
  383.8 6.2 %near_output.1.refs_4_ = f32[896,384]{1,0:T(8,128)S(1)} custom-call(s32[4]{0:T(128)S(1)} %pad_add_fusion.idx_ref, bf16[384,896]{1,0:T(8,128)(2,1)S(1)} %copy-done.12, bf16[896,3584]{1,0:T(8,128)(2,1)} %all-gather.11.cloned.1.call-done.refs_1_.refs_3_.refs_5_, bf16[384,896]{1,0:T(8,128)(2,1)} %collective-permute-done.24.refs_2_, ...), custom_call_target="tpu_custom_call" | custom-call | flops 1849688064 | bytes 9437184 | tf_op jit(solution)/shard_map/near_output/pallas_call | solution.py:553
  393.4 5.0 %collective-permute-done.27.refs_2_ = bf16[384,896]{1,0:T(8,128)(2,1)} collective-permute-done((bf16[384,896]{1,0:T(8,128)(2,1)}, bf16[384,896]{1,0:T(8,128)(2,1)}, u32[]{:S(2)}, u32[]{:S(2)}) %collective-permute-start.27) | collective-permute-done | bytes 688160 | tf_op jit(solution)/shard_map/ppermute | solution.py:139
  398.3 3.4 collective-permute-start.28
  403.0 5.2 %middle_output.1.refs_4_ = f32[896,384]{1,0:T(8,128)S(1)} custom-call(s32[4]{0:T(128)S(1)} %pad_add_fusion.idx_ref, bf16[384,896]{1,0:T(8,128)(2,1)} %collective-permute-done.25.refs_0_, bf16[896,3584]{1,0:T(8,128)(2,1)} %all-gather.11.cloned.1.call-done.refs_1_.refs_3_.refs_5_, bf16[384,896]{1,0:T(8,128)(2,1)} %collective-permute-done.27.refs_2_, ...), custom_call_target="tpu_custom_call" | custom-call | flops 1233125376 | bytes 6291456 | tf_op jit(solution)/shard_map/middle_output/pallas_call | solution.py:553
  409.4 4.9 %collective-permute-done.28.refs_0_ = bf16[384,896]{1,0:T(8,128)(2,1)} collective-permute-done((bf16[384,896]{1,0:T(8,128)(2,1)}, bf16[384,896]{1,0:T(8,128)(2,1)}, u32[]{:S(2)}, u32[]{:S(2)}) %collective-permute-start.28) | collective-permute-done | bytes 688160 | tf_op jit(solution)/shard_map/ppermute | solution.py:138
  414.2 4.9 %collective-permute-done.29.refs_2_ = bf16[384,896]{1,0:T(8,128)(2,1)} collective-permute-done((bf16[384,896]{1,0:T(8,128)(2,1)}, bf16[384,896]{1,0:T(8,128)(2,1)}, u32[]{:S(2)}, u32[]{:S(2)}) %collective-permute-start.29) | collective-permute-done | bytes 688160 | tf_op jit(solution)/shard_map/ppermute | solution.py:139
  419.2 5.6 %far_output.1 = bf16[896,384]{1,0:T(8,128)(2,1)S(1)} custom-call(s32[4]{0:T(128)S(1)} %pad_add_fusion.idx_ref, bf16[384,896]{1,0:T(8,128)(2,1)} %collective-permute-done.28.refs_0_, bf16[896,3584]{1,0:T(8,128)(2,1)} %all-gather.11.cloned.1.call-done.refs_1_.refs_3_.refs_5_, bf16[384,896]{1,0:T(8,128)(2,1)} %collective-permute-done.29.refs_2_, ...), custom_call_target="tpu_custom_call" | custom-call | flops 1233125376 | bytes 6291456 | tf_op jit(solution)/shard_map/far_output/pallas_call | solution.py:553
  425.6 3.7 collective-permute-start.32
  430.1 3.5 collective-permute-done.30.refs_1_
  433.6 5.0 %collective-permute-done.31.refs_2_ = bf16[224,384]{1,0:T(8,128)(2,1)S(1)} collective-permute-done((bf16[224,384]{1,0:T(8,128)(2,1)S(1)}, bf16[224,384]{1,0:T(8,128)(2,1)S(1)}, u32[]{:S(2)}, u32[]{:S(2)}) %collective-permute-start.31) | collective-permute-done | bytes 172064 | tf_op jit(solution)/shard_map/ppermute | solution.py:35
  (152 shorter events, 73.7 us)
Async XLA Ops:
  7.2 15.3 %copy-start = (bf16[4,128,3,896]{3,1,2,0:T(8,128)(2,1)S(1)}, bf16[4,128,3,896]{3,1,2,0:T(8,128)(2,1)}, u32[]{:S(2)}) copy-start(bf16[4,128,3,896]{3,1,2,0:T(8,128)(2,1)} %param.40) | copy-start | bytes 8257540
  7.2 107.3 %all-gather.5.cloned.1.call-start = ((), (), s32[]{:S(2)}) async-start(), calls=%async_computation.2 | async-start | bytes 7225344 | tf_op jit(solution)/shard_map/all_gather | solution.py:195
  16.2 27.9 %collective-permute-start = (bf16[112,2048]{1,0:T(8,128)(2,1)}, bf16[112,2048]{1,0:T(8,128)(2,1)}, u32[]{:S(2)}, u32[]{:S(2)}) collective-permute-start(bf16[112,2048]{1,0:T(8,128)(2,1)} %get-tuple-element.54), channel_id=1, source_target_pairs={{0,1},{1,0},{2,3},{3,2},{4,5},{5,4},{6,7},{7,6},{8,9},{9,8},{10,11... | collective-permute-start | bytes 1376264 | tf_op jit(solution)/shard_map/ppermute | solution.py:35
  19.3 34.3 %collective-permute-start.1 = (bf16[112,2048]{1,0:T(8,128)(2,1)}, bf16[112,2048]{1,0:T(8,128)(2,1)}, u32[]{:S(2)}, u32[]{:S(2)}) collective-permute-start(bf16[112,2048]{1,0:T(8,128)(2,1)} %get-tuple-element.55), channel_id=1, source_target_pairs={{0,2},{1,3},{2,0},{3,1},{4,6},{5,7},{6,4},{7,5},{8,10},{9,11},{10,... | collective-permute-start | bytes 1376264 | tf_op jit(solution)/shard_map/ppermute | solution.py:35
  21.9 31.7 %collective-permute-start.2 = (bf16[112,2048]{1,0:T(8,128)(2,1)}, bf16[112,2048]{1,0:T(8,128)(2,1)}, u32[]{:S(2)}, u32[]{:S(2)}) collective-permute-start(bf16[112,2048]{1,0:T(8,128)(2,1)} %get-tuple-element.56), channel_id=1, source_target_pairs={{0,3},{1,2},{2,1},{3,0},{4,7},{5,6},{6,5},{7,4},{8,11},{9,10},{10,... | collective-permute-start | bytes 1376264 | tf_op jit(solution)/shard_map/ppermute | solution.py:35
  27.8 4.8 %copy-start.27 = (f32[14]{0:T(128)S(1)}, f32[14]{0:T(128)}, u32[]{:S(2)}) copy-start(f32[14]{0:T(128)} %param.34) | copy-start | bytes 172
  40.8 14.3 %copy-start.6 = (bf16[8,384,448]{2,1,0:T(8,128)(2,1)}, bf16[8,384,448]{2,1,0:T(8,128)(2,1)S(1)}, u32[]{:S(2)}) copy-start(bf16[8,384,448]{2,1,0:T(8,128)(2,1)S(1)} %norm.1.act_ref) | copy-start | bytes 8257540
  55.0 3.9 collective-permute-start.5
  60.2 54.3 %all-to-all-start = ((bf16[4,224,896]{2,1,0:T(8,128)(2,1)}), bf16[4,224,896]{2,1,0:T(8,128)(2,1)}, u32[]{:S(2)}, u32[]{:S(2)}) async-start(bf16[4,224,896]{2,1,0:T(8,128)(2,1)} %copy-done.8), calls=%async_computation | async-start | bytes 3211264 | tf_op jit(solution)/shard_map/all_to_all | solution.py:104
  71.4 240.5 %all-gather.7.cloned.1.call-start = ((), (), s32[]{:S(2)}) async-start(), calls=%async_computation.3 | async-start | bytes 14450688 | tf_op jit(solution)/shard_map/all_gather | solution.py:195
  71.4 41.9 %collective-permute-start.3 = (bf16[448,2048]{1,0:T(8,128)(2,1)S(1)}, bf16[448,2048]{1,0:T(8,128)(2,1)}, u32[]{:S(2)}, u32[]{:S(2)}) collective-permute-start(bf16[448,2048]{1,0:T(8,128)(2,1)S(1)} %place.1.refs_0_), channel_id=1, source_target_pairs={{0,8},{4,12},{8,0},{12,4},{16,24},{20,28},{24,16},{28,20},{1,9},{5... | collective-permute-start | bytes 5505032 | tf_op jit(solution)/shard_map/ppermute | solution.py:35
  72.9 41.6 %collective-permute-start.4 = (bf16[448,2048]{1,0:T(8,128)(2,1)S(1)}, bf16[448,2048]{1,0:T(8,128)(2,1)}, u32[]{:S(2)}, u32[]{:S(2)}) collective-permute-start(bf16[448,2048]{1,0:T(8,128)(2,1)S(1)} %place.1.refs_0_), channel_id=1, source_target_pairs={{0,16},{4,20},{8,24},{12,28},{16,0},{20,4},{24,8},{28,12},{1,17},{... | collective-permute-start | bytes 5505032 | tf_op jit(solution)/shard_map/ppermute | solution.py:35
  114.6 93.5 %all-to-all-start.1 = ((bf16[4,224,1792]{2,1,0:T(8,128)(2,1)}), bf16[4,224,1792]{2,1,0:T(8,128)(2,1)}, u32[]{:S(2)}, u32[]{:S(2)}) async-start(bf16[4,224,1792]{2,1,0:T(8,128)(2,1)} %get-tuple-element.63), calls=%async_computation.1 | async-start | bytes 6422528 | tf_op jit(solution)/shard_map/all_to_all | solution.py:104
  119.4 215.5 %all-gather.9.cloned.1.call-start = ((), (), s32[]{:S(2)}) async-start(), calls=%async_computation.4 | async-start | bytes 28901376 | tf_op jit(solution)/shard_map/all_gather | solution.py:195
  121.2 38.3 %collective-permute-start.8 = (bf16[224,2048]{1,0:T(8,128)(2,1)S(1)}, bf16[224,2048]{1,0:T(8,128)(2,1)}, u32[]{:S(2)}, u32[]{:S(2)}) collective-permute-start(bf16[224,2048]{1,0:T(8,128)(2,1)S(1)} %slice.26), channel_id=1, source_target_pairs={{0,8},{4,12},{8,0},{12,4},{16,24},{20,28},{24,16},{28,20},{1,9},{5... | collective-permute-start | bytes 2752520 | tf_op jit(solution)/shard_map/ppermute | solution.py:35
  123.1 37.9 %collective-permute-start.9 = (bf16[224,2048]{1,0:T(8,128)(2,1)S(1)}, bf16[224,2048]{1,0:T(8,128)(2,1)}, u32[]{:S(2)}, u32[]{:S(2)}) collective-permute-start(bf16[224,2048]{1,0:T(8,128)(2,1)S(1)} %slice.27), channel_id=1, source_target_pairs={{0,16},{4,20},{8,24},{12,28},{16,0},{20,4},{24,8},{28,12},{1,17},{... | collective-permute-start | bytes 2752520 | tf_op jit(solution)/shard_map/ppermute | solution.py:35
  124.7 39.2 %collective-permute-start.6 = (bf16[448,2048]{1,0:T(8,128)(2,1)}, bf16[448,2048]{1,0:T(8,128)(2,1)}, u32[]{:S(2)}, u32[]{:S(2)}) collective-permute-start(bf16[448,2048]{1,0:T(8,128)(2,1)} %collective-permute-done.3.refs_2_), channel_id=1, source_target_pairs={{0,4},{4,0},{8,12},{12,8},{16,20},{20,16},{24,28},{28,24},{1,5},{5... | collective-permute-start | bytes 5505032 | tf_op jit(solution)/shard_map/ppermute | solution.py:35
  124.7 39.2 %collective-permute-start.7 = (bf16[448,2048]{1,0:T(8,128)(2,1)}, bf16[448,2048]{1,0:T(8,128)(2,1)}, u32[]{:S(2)}, u32[]{:S(2)}) collective-permute-start(bf16[448,2048]{1,0:T(8,128)(2,1)} %collective-permute-done.4.refs_3_), channel_id=1, source_target_pairs={{0,4},{4,0},{8,12},{12,8},{16,20},{20,16},{24,28},{28,24},{1,5},{5... | collective-permute-start | bytes 5505032 | tf_op jit(solution)/shard_map/ppermute | solution.py:35
  159.4 2.8 collective-permute-start.10
  161.1 2.8 collective-permute-start.11
  161.1 15.6 %copy-start.21 = (f32[4,128]{1,0:T(4,128)S(1)}, f32[4,128]{1,0:T(4,128)}, u32[]{:S(2)}) copy-start(f32[4,128]{1,0:T(4,128)} %bc_taps_ref.1) | copy-start | bytes 6148
  165.4 11.3 %copy-start.20 = (f32[4,896]{1,0:T(4,128)S(1)}, f32[4,896]{1,0:T(4,128)}, u32[]{:S(2)}) copy-start(f32[4,896]{1,0:T(4,128)} %taps_ref.1) | copy-start | bytes 43012
  183.9 19.9 %collective-permute-start.12 = (bf16[384,896]{1,0:T(8,128)(2,1)S(1)}, bf16[384,896]{1,0:T(8,128)(2,1)S(1)}, u32[]{:S(2)}, u32[]{:S(2)}) collective-permute-start(bf16[384,896]{1,0:T(8,128)(2,1)S(1)} %get-tuple-element.73.refs_0_), channel_id=1, source_target_pairs={{0,1},{1,2},{2,3},{4,5},{5,6},{6,7},{8,9},{9,10},{10,11},{12,13},{... | collective-permute-start | bytes 2064392 | tf_op jit(solution)/shard_map/ppermute | solution.py:138
  188.9 19.2 %collective-permute-start.13 = (bf16[384,896]{1,0:T(8,128)(2,1)S(1)}, bf16[384,896]{1,0:T(8,128)(2,1)}, u32[]{:S(2)}, u32[]{:S(2)}) collective-permute-start(bf16[384,896]{1,0:T(8,128)(2,1)S(1)} %get-tuple-element.73.refs_0_), channel_id=1, source_target_pairs={{1,0},{2,1},{3,2},{5,4},{6,5},{7,6},{9,8},{10,9},{11,10},{13,12},{... | collective-permute-start | bytes 2064392 | tf_op jit(solution)/shard_map/ppermute | solution.py:139
  208.1 174.6 %all-gather.11.cloned.1.call-start = ((), (), s32[]{:S(2)}) async-start(), calls=%async_computation.5 | async-start | bytes 7225344 | tf_op jit(solution)/shard_map/all_gather | solution.py:195
  208.1 17.3 %collective-permute-start.14 = (bf16[384,896]{1,0:T(8,128)(2,1)S(1)}, bf16[384,896]{1,0:T(8,128)(2,1)S(1)}, u32[]{:S(2)}, u32[]{:S(2)}) collective-permute-start(bf16[384,896]{1,0:T(8,128)(2,1)S(1)} %collective-permute-done.12.refs_3_), channel_id=1, source_target_pairs={{0,1},{1,2},{2,3},{4,5},{5,6},{6,7},{8,9},{9,10},{10,11},{12,13},{... | collective-permute-start | bytes 2064392 | tf_op jit(solution)/shard_map/ppermute | solution.py:138
  211.6 18.2 %collective-permute-start.15 = (bf16[384,896]{1,0:T(8,128)(2,1)}, bf16[384,896]{1,0:T(8,128)(2,1)S(1)}, u32[]{:S(2)}, u32[]{:S(2)}) collective-permute-start(bf16[384,896]{1,0:T(8,128)(2,1)} %collective-permute-done.13.refs_6_), channel_id=1, source_target_pairs={{1,0},{2,1},{3,2},{5,4},{6,5},{7,6},{9,8},{10,9},{11,10},{13,12},{... | collective-permute-start | bytes 2064392 | tf_op jit(solution)/shard_map/ppermute | solution.py:139
  229.8 15.4 %collective-permute-start.16 = (bf16[384,896]{1,0:T(8,128)(2,1)S(1)}, bf16[384,896]{1,0:T(8,128)(2,1)S(1)}, u32[]{:S(2)}, u32[]{:S(2)}) collective-permute-start(bf16[384,896]{1,0:T(8,128)(2,1)S(1)} %collective-permute-done.14.refs_0_), channel_id=1, source_target_pairs={{0,1},{1,2},{2,3},{4,5},{5,6},{6,7},{8,9},{9,10},{10,11},{12,13},{... | collective-permute-start | bytes 2064392 | tf_op jit(solution)/shard_map/ppermute | solution.py:138
  232.2 17.1 %collective-permute-start.17 = (bf16[384,896]{1,0:T(8,128)(2,1)S(1)}, bf16[384,896]{1,0:T(8,128)(2,1)S(1)}, u32[]{:S(2)}, u32[]{:S(2)}) collective-permute-start(bf16[384,896]{1,0:T(8,128)(2,1)S(1)} %collective-permute-done.15.refs_3_), channel_id=1, source_target_pairs={{1,0},{2,1},{3,2},{5,4},{6,5},{7,6},{9,8},{10,9},{11,10},{13,12},{... | collective-permute-start | bytes 2064392 | tf_op jit(solution)/shard_map/ppermute | solution.py:139
  254.3 16.3 %collective-permute-start.19 = (bf16[896,384]{1,0:T(8,128)(2,1)S(1)}, bf16[896,384]{1,0:T(8,128)(2,1)S(1)}, u32[]{:S(2)}, u32[]{:S(2)}) collective-permute-start(bf16[896,384]{1,0:T(8,128)(2,1)S(1)} %far_mixer.1.refs_5_), channel_id=1, source_target_pairs={{1,0},{2,1},{3,2},{5,4},{6,5},{7,6},{9,8},{10,9},{11,10},{13,12},{... | collective-permute-start | bytes 2064392 | tf_op jit(solution)/shard_map/ppermute | solution.py:139
  255.6 16.3 %collective-permute-start.18 = (bf16[896,384]{1,0:T(8,128)(2,1)S(1)}, bf16[896,384]{1,0:T(8,128)(2,1)S(1)}, u32[]{:S(2)}, u32[]{:S(2)}) collective-permute-start(bf16[896,384]{1,0:T(8,128)(2,1)S(1)} %far_mixer.1.refs_5_), channel_id=1, source_target_pairs={{0,1},{1,2},{2,3},{4,5},{5,6},{6,7},{8,9},{9,10},{10,11},{12,13},{... | collective-permute-start | bytes 2064392 | tf_op jit(solution)/shard_map/ppermute | solution.py:138
  270.5 15.5 %collective-permute-start.20 = (bf16[896,384]{1,0:T(8,128)(2,1)S(1)}, bf16[896,384]{1,0:T(8,128)(2,1)S(1)}, u32[]{:S(2)}, u32[]{:S(2)}) collective-permute-start(bf16[896,384]{1,0:T(8,128)(2,1)S(1)} %collective-permute-done.19), channel_id=1, source_target_pairs={{1,0},{2,1},{3,2},{5,4},{6,5},{7,6},{9,8},{10,9},{11,10},{13,12},{... | collective-permute-start | bytes 2064392 | tf_op jit(solution)/shard_map/ppermute | solution.py:139
  271.8 15.6 %collective-permute-start.22 = (bf16[896,384]{1,0:T(8,128)(2,1)S(1)}, bf16[896,384]{1,0:T(8,128)(2,1)S(1)}, u32[]{:S(2)}, u32[]{:S(2)}) collective-permute-start(bf16[896,384]{1,0:T(8,128)(2,1)S(1)} %collective-permute-done.18), channel_id=1, source_target_pairs={{0,1},{1,2},{2,3},{4,5},{5,6},{6,7},{8,9},{9,10},{10,11},{12,13},{... | collective-permute-start | bytes 2064392 | tf_op jit(solution)/shard_map/ppermute | solution.py:138
  286.0 14.8 %collective-permute-start.21 = (bf16[896,384]{1,0:T(8,128)(2,1)S(1)}, bf16[896,384]{1,0:T(8,128)(2,1)}, u32[]{:S(2)}, u32[]{:S(2)}) collective-permute-start(bf16[896,384]{1,0:T(8,128)(2,1)S(1)} %collective-permute-done.20), channel_id=1, source_target_pairs={{1,0},{2,1},{3,2},{5,4},{6,5},{7,6},{9,8},{10,9},{11,10},{13,12},{... | collective-permute-start | bytes 2064392 | tf_op jit(solution)/shard_map/ppermute | solution.py:139
  287.4 15.0 %collective-permute-start.23 = (bf16[896,384]{1,0:T(8,128)(2,1)S(1)}, bf16[896,384]{1,0:T(8,128)(2,1)S(1)}, u32[]{:S(2)}, u32[]{:S(2)}) collective-permute-start(bf16[896,384]{1,0:T(8,128)(2,1)S(1)} %collective-permute-done.22), channel_id=1, source_target_pairs={{0,1},{1,2},{2,3},{4,5},{5,6},{6,7},{8,9},{9,10},{10,11},{12,13},{... | collective-permute-start | bytes 2064392 | tf_op jit(solution)/shard_map/ppermute | solution.py:138
  334.9 17.3 %copy-start.13 = (bf16[384,896]{1,0:T(8,128)(2,1)S(1)}, bf16[384,896]{1,0:T(8,128)(2,1)}, u32[]{:S(2)}) copy-start(bf16[384,896]{1,0:T(8,128)(2,1)} %qkv.2.q_ref) | copy-start | bytes 2064388
  355.9 18.4 %collective-permute-start.24 = (bf16[384,896]{1,0:T(8,128)(2,1)S(1)}, bf16[384,896]{1,0:T(8,128)(2,1)}, u32[]{:S(2)}, u32[]{:S(2)}) collective-permute-start(bf16[384,896]{1,0:T(8,128)(2,1)S(1)} %attend.1.refs_0_), channel_id=1, source_target_pairs={{0,1},{1,2},{2,3},{4,5},{5,6},{6,7},{8,9},{9,10},{10,11},{12,13},{... | collective-permute-start | bytes 2064392 | tf_op jit(solution)/shard_map/ppermute | solution.py:138
  360.1 19.5 %collective-permute-start.26 = (bf16[384,896]{1,0:T(8,128)(2,1)S(1)}, bf16[384,896]{1,0:T(8,128)(2,1)}, u32[]{:S(2)}, u32[]{:S(2)}) collective-permute-start(bf16[384,896]{1,0:T(8,128)(2,1)S(1)} %attend.1.refs_0_), channel_id=1, source_target_pairs={{1,0},{2,1},{3,2},{5,4},{6,5},{7,6},{9,8},{10,9},{11,10},{13,12},{... | collective-permute-start | bytes 2064392 | tf_op jit(solution)/shard_map/ppermute | solution.py:139
  374.3 19.1 %collective-permute-start.25 = (bf16[384,896]{1,0:T(8,128)(2,1)}, bf16[384,896]{1,0:T(8,128)(2,1)}, u32[]{:S(2)}, u32[]{:S(2)}) collective-permute-start(bf16[384,896]{1,0:T(8,128)(2,1)} %collective-permute-done.24.refs_2_), channel_id=1, source_target_pairs={{0,1},{1,2},{2,3},{4,5},{5,6},{6,7},{8,9},{9,10},{10,11},{12,13},{... | collective-permute-start | bytes 2064392 | tf_op jit(solution)/shard_map/ppermute | solution.py:138
  379.6 18.7 %collective-permute-start.27 = (bf16[384,896]{1,0:T(8,128)(2,1)}, bf16[384,896]{1,0:T(8,128)(2,1)}, u32[]{:S(2)}, u32[]{:S(2)}) collective-permute-start(bf16[384,896]{1,0:T(8,128)(2,1)} %collective-permute-done.26.refs_4_), channel_id=1, source_target_pairs={{1,0},{2,1},{3,2},{5,4},{6,5},{7,6},{9,8},{10,9},{11,10},{13,12},{... | collective-permute-start | bytes 2064392 | tf_op jit(solution)/shard_map/ppermute | solution.py:139
  398.3 15.9 %collective-permute-start.28 = (bf16[384,896]{1,0:T(8,128)(2,1)}, bf16[384,896]{1,0:T(8,128)(2,1)}, u32[]{:S(2)}, u32[]{:S(2)}) collective-permute-start(bf16[384,896]{1,0:T(8,128)(2,1)} %collective-permute-done.25.refs_0_), channel_id=1, source_target_pairs={{0,1},{1,2},{2,3},{4,5},{5,6},{6,7},{8,9},{9,10},{10,11},{12,13},{... | collective-permute-start | bytes 2064392 | tf_op jit(solution)/shard_map/ppermute | solution.py:138
  401.7 17.5 %collective-permute-start.29 = (bf16[384,896]{1,0:T(8,128)(2,1)}, bf16[384,896]{1,0:T(8,128)(2,1)}, u32[]{:S(2)}, u32[]{:S(2)}) collective-permute-start(bf16[384,896]{1,0:T(8,128)(2,1)} %collective-permute-done.27.refs_2_), channel_id=1, source_target_pairs={{1,0},{2,1},{3,2},{5,4},{6,5},{7,6},{9,8},{10,9},{11,10},{13,12},{... | collective-permute-start | bytes 2064392 | tf_op jit(solution)/shard_map/ppermute | solution.py:139
  409.4 20.0 %copy-start.15 = (f32[896,64]{1,0:T(8,128)S(1)}, f32[896,64]{1,0:T(8,128)}, u32[]{:S(2)}) copy-start(f32[896,64]{1,0:T(8,128)} %copy-done.14) | copy-start | bytes 688132
  409.4 20.0 %copy-start.23 = (f32[1,14,64,64]{3,2,1,0:T(8,128)S(1)}, f32[1,14,64,64]{3,2,1,0:T(8,128)}, u32[]{:S(2)}) copy-start(f32[1,14,64,64]{3,2,1,0:T(8,128)} %param.26) | copy-start | bytes 688132
  419.2 21.2 %copy-start.1 = (bf16[4,128,3,896]{3,1,2,0:T(8,128)(2,1)S(1)}, bf16[4,128,3,896]{3,1,2,0:T(8,128)(2,1)}, u32[]{:S(2)}) copy-start(bf16[4,128,3,896]{3,1,2,0:T(8,128)(2,1)} %param.40) | copy-start | bytes 8257540
  424.8 8.8 %collective-permute-start.30 = (bf16[224,384]{1,0:T(8,128)(2,1)S(1)}, bf16[224,384]{1,0:T(8,128)(2,1)S(1)}, u32[]{:S(2)}, u32[]{:S(2)}) collective-permute-start(bf16[224,384]{1,0:T(8,128)(2,1)S(1)} %get-tuple-element.106), channel_id=1, source_target_pairs={{0,1},{1,0},{2,3},{3,2},{4,5},{5,4},{6,7},{7,6},{8,9},{9,8},{10,11... | collective-permute-start | bytes 516104 | tf_op jit(solution)/shard_map/ppermute | solution.py:35
  425.6 13.0 %collective-permute-start.31 = (bf16[224,384]{1,0:T(8,128)(2,1)S(1)}, bf16[224,384]{1,0:T(8,128)(2,1)S(1)}, u32[]{:S(2)}, u32[]{:S(2)}) collective-permute-start(bf16[224,384]{1,0:T(8,128)(2,1)S(1)} %get-tuple-element.105), channel_id=1, source_target_pairs={{0,2},{1,3},{2,0},{3,1},{4,6},{5,7},{6,4},{7,5},{8,10},{9,11},{10,... | collective-permute-start | bytes 516104 | tf_op jit(solution)/shard_map/ppermute | solution.py:35
  425.6 13.0 %collective-permute-start.32 = (bf16[224,384]{1,0:T(8,128)(2,1)S(1)}, bf16[224,384]{1,0:T(8,128)(2,1)S(1)}, u32[]{:S(2)}, u32[]{:S(2)}) collective-permute-start(bf16[224,384]{1,0:T(8,128)(2,1)S(1)} %get-tuple-element.104), channel_id=1, source_target_pairs={{0,3},{1,2},{2,1},{3,0},{4,7},{5,6},{6,5},{7,4},{8,11},{9,10},{10,... | collective-permute-start | bytes 516104 | tf_op jit(solution)/shard_map/ppermute | solution.py:35
  (21 other events, 47.1 us)
Sparse Core Ops, SparseCore 0:
  9.9 49.4 all-gather.4
  114.7 90.0 all-gather.6
  208.2 126.6 all-gather.8
  336.6 46.0 all-gather.10

commit v2 on v1

--- a/solution.py
+++ b/solution.py
@@ -766,7 +766,6 @@
     ups, per_head = early[5:7], early[7:]
     zx_gather = Gather(zx_own)
     zx_first = zx_gather.first()
-    q_send, zx_gather.core = after([q_send, zx_gather.core], [])
     q_own = tp_trade(q_send)
     gain_all = zx_own.reshape(tp_count, rows, -1)[:, :, 2 * inner + used :].astype(F32)
     gain_all = (gain_all[:, :, :each] + gain_all[:, :, each : 2 * each]).reshape(tp_count, 1, inner)

time: 453 us -> 447 us (0.987)
    unnamed x62 -> x58, local copies, waits for them, and re-layouts: 21.5 us -> 18.7 us
  transfers between devices with their start and end apart: 39 -> 39, of which waited for: 26 -> 25; matrix products, arithmetic and copies ran while one was open for 5% -> 5% of each run, Pallas kernels for 20% -> 21%
where the time goes in v2:
time: 447 us; the launch traced here: 441 us
  waiting for transfers between devices  203 us (45%)
  Pallas kernels  99.1 us (22%)
  starting transfers between devices  82.2 us (18%)
  local copies, waits for them, and re-layouts  31.8 us (7%)
  between operations  16.7 us (4%)
  other arithmetic  8.18 us (2%)
    ppermute x15, waiting for transfers between devices, exchange(): return lax.ppermute(value, axis, [(i, i ^ bits) for i in range(count)])  96.7 us
    ppermute x9, waiting for transfers between devices, tp_step(): lax.ppermute(pair[1], 'tp', [(i + 1, i) for i in range(count - 1)])  50.4 us
    ppermute x9, waiting for transfers between devices, tp_step(): lax.ppermute(pair[0], 'tp', [(i, i + 1) for i in range(count - 1)])  42.1 us
    ppermute x9, starting transfers between devices, tp_step(): lax.ppermute(pair[0], 'tp', [(i, i + 1) for i in range(count - 1)])  37.7 us
    pallas_call x6, Pallas kernels, run(): pl.pallas_call(partial(columns_kernel, scaled, steps, not begun, last, sh...  34.1 us
    pallas_call x2, Pallas kernels, rows_matmul(): pl.pallas_call(rows_kernel, grid=(owners,), in_specs=[pl.BlockSpec((1, to...  28.3 us
    unnamed x58, local copies, waits for them, and re-layouts  18.7 us
    all_to_all x2, starting transfers between devices, tp_trade(): out = lax.all_to_all(slices, 'tp', split_axis=0, concat_axis=0, tiled=True)  16.1 us
  transfers between devices with their start and end apart: 39, of which 25 were waited for; matrix products, arithmetic and copies ran while one was open for 5% of the time, Pallas kernels for 21%

profile of v2, /device:TPU:0, one launch (start us, length us, event | category | flops | bytes accessed | tf_op | source)
XLA Modules:
  0.0 440.7 jit_solution(12069256971263996339)
XLA Ops:
  7.2 2.6 convert_bitcast_fusion
  16.2 3.0 collective-permute-start
  19.3 2.6 collective-permute-start.1
  27.8 2.8 copy.45
  32.9 3.7 copy-done.3
  36.6 2.7 prepare.1
  44.2 9.4 %collective-permute-done.1.refs_2_ = bf16[112,2048]{1,0:T(8,128)(2,1)} collective-permute-done((bf16[112,2048]{1,0:T(8,128)(2,1)}, bf16[112,2048]{1,0:T(8,128)(2,1)}, u32[]{:S(2)}, u32[]{:S(2)}) %collective-permute-start.1) | collective-permute-done | bytes 458784 | tf_op jit(solution)/shard_map/ppermute | solution.py:35
  55.0 11.3 %all-to-all-start = ((bf16[4,224,896]{2,1,0:T(8,128)(2,1)}), bf16[4,224,896]{2,1,0:T(8,128)(2,1)}, u32[]{:S(2)}, u32[]{:S(2)}) async-start(bf16[4,224,896]{2,1,0:T(8,128)(2,1)} %copy-done.8), calls=%async_computation | async-start | bytes 3211264 | tf_op jit(solution)/shard_map/all_to_all | solution.py:104
  69.7 37.0 %collective-permute-done.3.refs_2_ = bf16[448,2048]{1,0:T(8,128)(2,1)} collective-permute-done((bf16[448,2048]{1,0:T(8,128)(2,1)S(1)}, bf16[448,2048]{1,0:T(8,128)(2,1)}, u32[]{:S(2)}, u32[]{:S(2)}) %collective-permute-start.3) | collective-permute-done | bytes 1835040 | tf_op jit(solution)/shard_map/ppermute | solution.py:35
  108.0 4.9 %all-to-all-start.1 = ((bf16[4,224,1792]{2,1,0:T(8,128)(2,1)}), bf16[4,224,1792]{2,1,0:T(8,128)(2,1)}, u32[]{:S(2)}, u32[]{:S(2)}) async-start(bf16[4,224,1792]{2,1,0:T(8,128)(2,1)} %get-tuple-element.60), calls=%async_computation.1 | async-start | bytes 6422528 | tf_op jit(solution)/shard_map/all_to_all | solution.py:104
  118.7 36.1 %collective-permute-done.8.refs_6_ = bf16[224,2048]{1,0:T(8,128)(2,1)} collective-permute-done((bf16[224,2048]{1,0:T(8,128)(2,1)S(1)}, bf16[224,2048]{1,0:T(8,128)(2,1)}, u32[]{:S(2)}, u32[]{:S(2)}) %collective-permute-start.8) | collective-permute-done | bytes 917536 | tf_op jit(solution)/shard_map/ppermute | solution.py:35
  159.3 11.7 %zx.1.zx_ref = bf16[384,2048]{1,0:T(8,128)(2,1)S(1)} custom-call(s32[1]{0:T(128)} %bitcast.req_ref, bf16[8,384,448]{2,1,0:T(8,128)(2,1)} %copy-done.6, bf16[448,2048]{1,0:T(8,128)(2,1)S(1)} %place.1.refs_0_, bf16[448,2048]{1,0:T(8,128)(2,1)} %collective-permute-done.5.refs_1_, bf16[448,2048]{1,0:T(8,128)(2,1)} %collective-permute-done.3.refs_2_, ...), custom_call_target="tpu_custom_call" | custom-call | flops 5637144576 | bytes 14680064 | tf_op jit(solution)/shard_map/zx/pallas_call | solution.py:287
  171.1 6.4 %scan.1 = (bf16[384,896]{1,0:T(8,128)(2,1)S(1)}, f32[896,64]{1,0:T(8,128)S(1)}) custom-call(s32[2]{0:T(128)S(1)} %pad_add_fusion.1.info_ref, bf16[384,2048]{1,0:T(8,128)(2,1)S(1)} %zx.1.zx_ref, f32[4,896]{1,0:T(4,128)S(1)} %copy-done.18, f32[4,128]{1,0:T(4,128)S(1)} %copy-done.19, f32[1,128]{1,0:T(1,128)S(1)} %pad.19.bias_ref, f32[16,1]{1,0:T(8,128)S(1)} %pad.20.bias_t_ref, ...), custom_call_target="tpu_custom_call" | custom-call | flops 6000000000 | bytes 4194304 | tf_op jit(solution)/shard_map/scan/pallas_call | solution.py:445
  178.3 4.0 collective-permute-start.12
  183.6 13.6 %collective-permute-done.12.refs_3_ = bf16[384,896]{1,0:T(8,128)(2,1)S(1)} collective-permute-done((bf16[384,896]{1,0:T(8,128)(2,1)S(1)}, bf16[384,896]{1,0:T(8,128)(2,1)S(1)}, u32[]{:S(2)}, u32[]{:S(2)}) %collective-permute-start.12) | collective-permute-done | bytes 688160 | tf_op jit(solution)/shard_map/ppermute | solution.py:138
  197.3 4.3 collective-permute-done.13.refs_6_
  201.6 3.5 collective-permute-start.14
  206.6 7.3 %near_mixer.1 = (f32[896,384]{1,0:T(8,128)S(1)}, f32[384,128]{1,0:T(8,128)S(1)}) custom-call(s32[4]{0:T(128)S(1)} %pad_add_fusion.idx_ref, bf16[384,896]{1,0:T(8,128)(2,1)S(1)} %get-tuple-element.69.refs_0_, bf16[896,3584]{1,0:T(8,128)(2,1)} %all-gather.5.cloned.1.call-done.refs_1_.refs_4_.refs_7_, f32[4,1,896]{2,1,0:T(1,128)S(1)} %copy.49.refs_2_.refs_5_.refs_8_, ...), custom_call_target="tpu_custom_call" | custom-call | flops 1849688064 | bytes 9437184 | tf_op jit(solution)/shard_map/near_mixer/pallas_call | solution.py:553
  215.0 3.9 collective-permute-done.14.refs_0_
  218.8 4.4 collective-permute-done.15.refs_3_
  223.2 3.2 collective-permute-start.16
  227.7 4.9 %middle_mixer.1 = (f32[896,384]{1,0:T(8,128)S(1)}, f32[384,128]{1,0:T(8,128)S(1)}) custom-call(s32[4]{0:T(128)S(1)} %pad_add_fusion.idx_ref, bf16[384,896]{1,0:T(8,128)(2,1)S(1)} %collective-permute-done.14.refs_0_, bf16[896,3584]{1,0:T(8,128)(2,1)} %all-gather.5.cloned.1.call-done.refs_1_.refs_4_.refs_7_, f32[4,1,896]{2,1,0:T(1,128)S(1)} %copy.49.refs_2_.refs_5_.refs_8_, ...), custom_call_target="tpu_custom_call" | custom-call | flops 1233125376 | bytes 6291456 | tf_op jit(solution)/shard_map/middle_mixer/pallas_call | solution.py:553
  233.8 5.4 %collective-permute-done.16.refs_0_ = bf16[384,896]{1,0:T(8,128)(2,1)S(1)} collective-permute-done((bf16[384,896]{1,0:T(8,128)(2,1)S(1)}, bf16[384,896]{1,0:T(8,128)(2,1)S(1)}, u32[]{:S(2)}, u32[]{:S(2)}) %collective-permute-start.16) | collective-permute-done | bytes 688160 | tf_op jit(solution)/shard_map/ppermute | solution.py:138
  239.1 4.2 collective-permute-done.17.refs_3_
  243.3 4.9 %far_mixer.1.refs_5_ = bf16[896,384]{1,0:T(8,128)(2,1)S(1)} custom-call(s32[4]{0:T(128)S(1)} %pad_add_fusion.idx_ref, bf16[384,896]{1,0:T(8,128)(2,1)S(1)} %collective-permute-done.16.refs_0_, bf16[896,3584]{1,0:T(8,128)(2,1)} %all-gather.5.cloned.1.call-done.refs_1_.refs_4_.refs_7_, f32[4,1,896]{2,1,0:T(1,128)S(1)} %copy.49.refs_2_.refs_5_.refs_8_, ...), custom_call_target="tpu_custom_call" | custom-call | flops 1233125376 | bytes 6291456 | tf_op jit(solution)/shard_map/far_mixer/pallas_call | solution.py:553
  249.5 4.6 %collective-permute-start.18 = (bf16[896,384]{1,0:T(8,128)(2,1)S(1)}, bf16[896,384]{1,0:T(8,128)(2,1)S(1)}, u32[]{:S(2)}, u32[]{:S(2)}) collective-permute-start(bf16[896,384]{1,0:T(8,128)(2,1)S(1)} %far_mixer.1.refs_5_), channel_id=1, source_target_pairs={{0,1},{1,2},{2,3},{4,5},{5,6},{6,7},{8,9},{9,10},{10,11},{12,13},{... | collective-permute-start | bytes 2064392 | tf_op jit(solution)/shard_map/ppermute | solution.py:138
  254.1 10.1 %collective-permute-done.19 = bf16[896,384]{1,0:T(8,128)(2,1)S(1)} collective-permute-done((bf16[896,384]{1,0:T(8,128)(2,1)S(1)}, bf16[896,384]{1,0:T(8,128)(2,1)S(1)}, u32[]{:S(2)}, u32[]{:S(2)}) %collective-permute-start.19) | collective-permute-done | bytes 688160 | tf_op jit(solution)/shard_map/ppermute | solution.py:139
  265.5 4.6 %collective-permute-start.22 = (bf16[896,384]{1,0:T(8,128)(2,1)S(1)}, bf16[896,384]{1,0:T(8,128)(2,1)S(1)}, u32[]{:S(2)}, u32[]{:S(2)}) collective-permute-start(bf16[896,384]{1,0:T(8,128)(2,1)S(1)} %collective-permute-done.18), channel_id=1, source_target_pairs={{0,1},{1,2},{2,3},{4,5},{5,6},{6,7},{8,9},{9,10},{10,11},{12,13},{... | collective-permute-start | bytes 2064392 | tf_op jit(solution)/shard_map/ppermute | solution.py:138
  270.1 9.6 %collective-permute-done.20 = bf16[896,384]{1,0:T(8,128)(2,1)S(1)} collective-permute-done((bf16[896,384]{1,0:T(8,128)(2,1)S(1)}, bf16[896,384]{1,0:T(8,128)(2,1)S(1)}, u32[]{:S(2)}, u32[]{:S(2)}) %collective-permute-start.20) | collective-permute-done | bytes 688160 | tf_op jit(solution)/shard_map/ppermute | solution.py:139
  281.1 4.8 %collective-permute-start.23 = (bf16[896,384]{1,0:T(8,128)(2,1)S(1)}, bf16[896,384]{1,0:T(8,128)(2,1)S(1)}, u32[]{:S(2)}, u32[]{:S(2)}) collective-permute-start(bf16[896,384]{1,0:T(8,128)(2,1)S(1)} %collective-permute-done.22), channel_id=1, source_target_pairs={{0,1},{1,2},{2,3},{4,5},{5,6},{6,7},{8,9},{9,10},{10,11},{12,13},{... | collective-permute-start | bytes 2064392 | tf_op jit(solution)/shard_map/ppermute | solution.py:138
  286.3 8.0 %collective-permute-done.21 = bf16[896,384]{1,0:T(8,128)(2,1)} collective-permute-done((bf16[896,384]{1,0:T(8,128)(2,1)S(1)}, bf16[896,384]{1,0:T(8,128)(2,1)}, u32[]{:S(2)}, u32[]{:S(2)}) %collective-permute-start.21) | collective-permute-done | bytes 688160 | tf_op jit(solution)/shard_map/ppermute | solution.py:139
  297.9 6.9 %join.1 = (bf16[4,384,1792]{2,1,0:T(8,128)(2,1)}, bf16[384,128]{1,0:T(8,128)(2,1)S(1)}) custom-call(s32[1]{0:T(128)} %copy.66.which_ref, bf16[3584,384]{1,0:T(8,128)(2,1)S(1)} %bitcast.63, bf16[384,3584]{1,0:T(8,128)(2,1)S(1)} %bitcast.67, f32[1,7168]{1,0:T(1,128)S(1)} %bitcast.70, bf16[4,7168,128]{2,1,0:T(8,128)(2,1)} %down_ref.1), custom_call_target="tpu_custom_call" | custom-call | flops 704643072 | bytes 13631488 | tf_op jit(solution)/shard_map/join/pallas_call | solution.py:603
  305.4 11.0 %qkv.2.q_ref = bf16[384,896]{1,0:T(8,128)(2,1)} custom-call(bf16[4,384,1792]{2,1,0:T(8,128)(2,1)} %get-tuple-element.83.act_ref, bf16[7168,896]{1,0:T(8,128)(2,1)} %all-gather.7.cloned.1.call-done.w_ref, bf16[384,128]{1,0:T(8,128)(2,1)} %copy-done.16, bf16[128,896]{1,0:T(8,128)(2,1)} %slice_bitcast_fusion.1.up_ref), custom_call_target="tpu_custom_call" | custom-call | flops 4932501504 | bytes 12845056 | tf_op jit(solution)/shard_map/qkv/pallas_call | solution.py:324
  316.4 11.8 %all-gather.9.cloned.1.call-done.w_ref = bf16[7168,1792]{1,0:T(8,128)(2,1)} async-done(((bf16[896,1792]{1,0:T(8,128)(2,1)}), bf16[7168,1792]{1,0:T(8,128)(2,1)}) %all-gather.9.cloned.1.call-update) | async-done | bytes 25690128 | tf_op jit(solution)/shard_map/all_gather | solution.py:195
  328.3 17.2 %qkv.3.kv_ref = bf16[384,1792]{1,0:T(8,128)(2,1)} custom-call(bf16[4,384,1792]{2,1,0:T(8,128)(2,1)} %get-tuple-element.83.act_ref, bf16[7168,1792]{1,0:T(8,128)(2,1)} %all-gather.9.cloned.1.call-done.w_ref, bf16[384,128]{1,0:T(8,128)(2,1)} %copy-done.16, bf16[128,1792]{1,0:T(8,128)(2,1)} %bitcast.74), custom_call_target="tpu_custom_call" | custom-call | flops 9865003008 | bytes 25690112 | tf_op jit(solution)/shard_map/qkv/pallas_call | solution.py:324
  349.2 4.2 collective-permute-start.24
  355.6 12.1 %collective-permute-done.24.refs_2_ = bf16[384,896]{1,0:T(8,128)(2,1)} collective-permute-done((bf16[384,896]{1,0:T(8,128)(2,1)S(1)}, bf16[384,896]{1,0:T(8,128)(2,1)}, u32[]{:S(2)}, u32[]{:S(2)}) %collective-permute-start.24) | collective-permute-done | bytes 688160 | tf_op jit(solution)/shard_map/ppermute | solution.py:138
  367.7 5.4 %collective-permute-start.25 = (bf16[384,896]{1,0:T(8,128)(2,1)}, bf16[384,896]{1,0:T(8,128)(2,1)}, u32[]{:S(2)}, u32[]{:S(2)}) collective-permute-start(bf16[384,896]{1,0:T(8,128)(2,1)} %collective-permute-done.24.refs_2_), channel_id=1, source_target_pairs={{0,1},{1,2},{2,3},{4,5},{5,6},{6,7},{8,9},{9,10},{10,11},{12,13},{... | collective-permute-start | bytes 2064392 | tf_op jit(solution)/shard_map/ppermute | solution.py:138
  377.2 6.2 %near_output.1.refs_4_ = f32[896,384]{1,0:T(8,128)S(1)} custom-call(s32[4]{0:T(128)S(1)} %pad_add_fusion.idx_ref, bf16[384,896]{1,0:T(8,128)(2,1)S(1)} %copy-done.12, bf16[896,3584]{1,0:T(8,128)(2,1)} %all-gather.11.cloned.1.call-done.refs_1_.refs_3_.refs_5_, bf16[384,896]{1,0:T(8,128)(2,1)} %collective-permute-done.24.refs_2_, ...), custom_call_target="tpu_custom_call" | custom-call | flops 1849688064 | bytes 9437184 | tf_op jit(solution)/shard_map/near_output/pallas_call | solution.py:553
  386.8 5.0 %collective-permute-done.27.refs_2_ = bf16[384,896]{1,0:T(8,128)(2,1)} collective-permute-done((bf16[384,896]{1,0:T(8,128)(2,1)}, bf16[384,896]{1,0:T(8,128)(2,1)}, u32[]{:S(2)}, u32[]{:S(2)}) %collective-permute-start.27) | collective-permute-done | bytes 688160 | tf_op jit(solution)/shard_map/ppermute | solution.py:139
  391.7 3.4 collective-permute-start.28
  396.5 5.2 %middle_output.1.refs_4_ = f32[896,384]{1,0:T(8,128)S(1)} custom-call(s32[4]{0:T(128)S(1)} %pad_add_fusion.idx_ref, bf16[384,896]{1,0:T(8,128)(2,1)} %collective-permute-done.25.refs_0_, bf16[896,3584]{1,0:T(8,128)(2,1)} %all-gather.11.cloned.1.call-done.refs_1_.refs_3_.refs_5_, bf16[384,896]{1,0:T(8,128)(2,1)} %collective-permute-done.27.refs_2_, ...), custom_call_target="tpu_custom_call" | custom-call | flops 1233125376 | bytes 6291456 | tf_op jit(solution)/shard_map/middle_output/pallas_call | solution.py:553
  402.8 4.9 %collective-permute-done.28.refs_0_ = bf16[384,896]{1,0:T(8,128)(2,1)} collective-permute-done((bf16[384,896]{1,0:T(8,128)(2,1)}, bf16[384,896]{1,0:T(8,128)(2,1)}, u32[]{:S(2)}, u32[]{:S(2)}) %collective-permute-start.28) | collective-permute-done | bytes 688160 | tf_op jit(solution)/shard_map/ppermute | solution.py:138
  407.7 5.0 %collective-permute-done.29.refs_2_ = bf16[384,896]{1,0:T(8,128)(2,1)} collective-permute-done((bf16[384,896]{1,0:T(8,128)(2,1)}, bf16[384,896]{1,0:T(8,128)(2,1)}, u32[]{:S(2)}, u32[]{:S(2)}) %collective-permute-start.29) | collective-permute-done | bytes 688160 | tf_op jit(solution)/shard_map/ppermute | solution.py:139
  412.7 5.6 %far_output.1 = bf16[896,384]{1,0:T(8,128)(2,1)S(1)} custom-call(s32[4]{0:T(128)S(1)} %pad_add_fusion.idx_ref, bf16[384,896]{1,0:T(8,128)(2,1)} %collective-permute-done.28.refs_0_, bf16[896,3584]{1,0:T(8,128)(2,1)} %all-gather.11.cloned.1.call-done.refs_1_.refs_3_.refs_5_, bf16[384,896]{1,0:T(8,128)(2,1)} %collective-permute-done.29.refs_2_, ...), custom_call_target="tpu_custom_call" | custom-call | flops 1233125376 | bytes 6291456 | tf_op jit(solution)/shard_map/far_output/pallas_call | solution.py:553
  419.0 3.8 collective-permute-start.32
  423.6 3.4 collective-permute-done.30.refs_1_
  427.0 5.1 %collective-permute-done.31.refs_2_ = bf16[224,384]{1,0:T(8,128)(2,1)S(1)} collective-permute-done((bf16[224,384]{1,0:T(8,128)(2,1)S(1)}, bf16[224,384]{1,0:T(8,128)(2,1)S(1)}, u32[]{:S(2)}, u32[]{:S(2)}) %collective-permute-start.31) | collective-permute-done | bytes 172064 | tf_op jit(solution)/shard_map/ppermute | solution.py:35
  (148 shorter events, 68.4 us)
Async XLA Ops:
  7.2 15.4 %copy-start = (bf16[4,128,3,896]{3,1,2,0:T(8,128)(2,1)S(1)}, bf16[4,128,3,896]{3,1,2,0:T(8,128)(2,1)}, u32[]{:S(2)}) copy-start(bf16[4,128,3,896]{3,1,2,0:T(8,128)(2,1)} %param.40) | copy-start | bytes 8257540
  7.2 100.8 %all-gather.5.cloned.1.call-start = ((), (), s32[]{:S(2)}) async-start(), calls=%async_computation.2 | async-start | bytes 7225344 | tf_op jit(solution)/shard_map/all_gather | solution.py:195
  16.2 27.9 %collective-permute-start = (bf16[112,2048]{1,0:T(8,128)(2,1)}, bf16[112,2048]{1,0:T(8,128)(2,1)}, u32[]{:S(2)}, u32[]{:S(2)}) collective-permute-start(bf16[112,2048]{1,0:T(8,128)(2,1)} %get-tuple-element.52), channel_id=1, source_target_pairs={{0,1},{1,0},{2,3},{3,2},{4,5},{5,4},{6,7},{7,6},{8,9},{9,8},{10,11... | collective-permute-start | bytes 1376264 | tf_op jit(solution)/shard_map/ppermute | solution.py:35
  19.3 34.3 %collective-permute-start.1 = (bf16[112,2048]{1,0:T(8,128)(2,1)}, bf16[112,2048]{1,0:T(8,128)(2,1)}, u32[]{:S(2)}, u32[]{:S(2)}) collective-permute-start(bf16[112,2048]{1,0:T(8,128)(2,1)} %get-tuple-element.53), channel_id=1, source_target_pairs={{0,2},{1,3},{2,0},{3,1},{4,6},{5,7},{6,4},{7,5},{8,10},{9,11},{10,... | collective-permute-start | bytes 1376264 | tf_op jit(solution)/shard_map/ppermute | solution.py:35
  21.9 31.7 %collective-permute-start.2 = (bf16[112,2048]{1,0:T(8,128)(2,1)}, bf16[112,2048]{1,0:T(8,128)(2,1)}, u32[]{:S(2)}, u32[]{:S(2)}) collective-permute-start(bf16[112,2048]{1,0:T(8,128)(2,1)} %get-tuple-element.54), channel_id=1, source_target_pairs={{0,3},{1,2},{2,1},{3,0},{4,7},{5,6},{6,5},{7,4},{8,11},{9,10},{10,... | collective-permute-start | bytes 1376264 | tf_op jit(solution)/shard_map/ppermute | solution.py:35
  27.8 4.9 %copy-start.25 = (f32[14]{0:T(128)S(1)}, f32[14]{0:T(128)}, u32[]{:S(2)}) copy-start(f32[14]{0:T(128)} %param.34) | copy-start | bytes 172
  40.8 14.2 %copy-start.6 = (bf16[8,384,448]{2,1,0:T(8,128)(2,1)}, bf16[8,384,448]{2,1,0:T(8,128)(2,1)S(1)}, u32[]{:S(2)}) copy-start(bf16[8,384,448]{2,1,0:T(8,128)(2,1)S(1)} %norm.1.act_ref) | copy-start | bytes 8257540
  55.0 52.9 %all-to-all-start = ((bf16[4,224,896]{2,1,0:T(8,128)(2,1)}), bf16[4,224,896]{2,1,0:T(8,128)(2,1)}, u32[]{:S(2)}, u32[]{:S(2)}) async-start(bf16[4,224,896]{2,1,0:T(8,128)(2,1)} %copy-done.8), calls=%async_computation | async-start | bytes 3211264 | tf_op jit(solution)/shard_map/all_to_all | solution.py:104
  66.3 239.1 %all-gather.7.cloned.1.call-start = ((), (), s32[]{:S(2)}) async-start(), calls=%async_computation.3 | async-start | bytes 14450688 | tf_op jit(solution)/shard_map/all_gather | solution.py:195
  66.3 40.4 %collective-permute-start.3 = (bf16[448,2048]{1,0:T(8,128)(2,1)S(1)}, bf16[448,2048]{1,0:T(8,128)(2,1)}, u32[]{:S(2)}, u32[]{:S(2)}) collective-permute-start(bf16[448,2048]{1,0:T(8,128)(2,1)S(1)} %place.1.refs_0_), channel_id=1, source_target_pairs={{0,8},{4,12},{8,0},{12,4},{16,24},{20,28},{24,16},{28,20},{1,9},{5... | collective-permute-start | bytes 5505032 | tf_op jit(solution)/shard_map/ppermute | solution.py:35
  67.8 40.2 %collective-permute-start.4 = (bf16[448,2048]{1,0:T(8,128)(2,1)S(1)}, bf16[448,2048]{1,0:T(8,128)(2,1)}, u32[]{:S(2)}, u32[]{:S(2)}) collective-permute-start(bf16[448,2048]{1,0:T(8,128)(2,1)S(1)} %place.1.refs_0_), channel_id=1, source_target_pairs={{0,16},{4,20},{8,24},{12,28},{16,0},{20,4},{24,8},{28,12},{1,17},{... | collective-permute-start | bytes 5505032 | tf_op jit(solution)/shard_map/ppermute | solution.py:35
  108.0 93.5 %all-to-all-start.1 = ((bf16[4,224,1792]{2,1,0:T(8,128)(2,1)}), bf16[4,224,1792]{2,1,0:T(8,128)(2,1)}, u32[]{:S(2)}, u32[]{:S(2)}) async-start(bf16[4,224,1792]{2,1,0:T(8,128)(2,1)} %get-tuple-element.60), calls=%async_computation.1 | async-start | bytes 6422528 | tf_op jit(solution)/shard_map/all_to_all | solution.py:104
  112.8 215.4 %all-gather.9.cloned.1.call-start = ((), (), s32[]{:S(2)}) async-start(), calls=%async_computation.4 | async-start | bytes 28901376 | tf_op jit(solution)/shard_map/all_gather | solution.py:195
  113.4 43.2 %collective-permute-start.5 = (bf16[448,2048]{1,0:T(8,128)(2,1)S(1)}, bf16[448,2048]{1,0:T(8,128)(2,1)}, u32[]{:S(2)}, u32[]{:S(2)}) collective-permute-start(bf16[448,2048]{1,0:T(8,128)(2,1)S(1)} %place.1.refs_0_), channel_id=1, source_target_pairs={{0,4},{4,0},{8,12},{12,8},{16,20},{20,16},{24,28},{28,24},{1,5},{5... | collective-permute-start | bytes 5505032 | tf_op jit(solution)/shard_map/ppermute | solution.py:35
  114.7 40.2 %collective-permute-start.8 = (bf16[224,2048]{1,0:T(8,128)(2,1)S(1)}, bf16[224,2048]{1,0:T(8,128)(2,1)}, u32[]{:S(2)}, u32[]{:S(2)}) collective-permute-start(bf16[224,2048]{1,0:T(8,128)(2,1)S(1)} %slice.26), channel_id=1, source_target_pairs={{0,8},{4,12},{8,0},{12,4},{16,24},{20,28},{24,16},{28,20},{1,9},{5... | collective-permute-start | bytes 2752520 | tf_op jit(solution)/shard_map/ppermute | solution.py:35
  116.7 39.8 %collective-permute-start.9 = (bf16[224,2048]{1,0:T(8,128)(2,1)S(1)}, bf16[224,2048]{1,0:T(8,128)(2,1)}, u32[]{:S(2)}, u32[]{:S(2)}) collective-permute-start(bf16[224,2048]{1,0:T(8,128)(2,1)S(1)} %slice.27), channel_id=1, source_target_pairs={{0,16},{4,20},{8,24},{12,28},{16,0},{20,4},{24,8},{28,12},{1,17},{... | collective-permute-start | bytes 2752520 | tf_op jit(solution)/shard_map/ppermute | solution.py:35
  118.2 41.1 %collective-permute-start.6 = (bf16[448,2048]{1,0:T(8,128)(2,1)}, bf16[448,2048]{1,0:T(8,128)(2,1)}, u32[]{:S(2)}, u32[]{:S(2)}) collective-permute-start(bf16[448,2048]{1,0:T(8,128)(2,1)} %collective-permute-done.3.refs_2_), channel_id=1, source_target_pairs={{0,4},{4,0},{8,12},{12,8},{16,20},{20,16},{24,28},{28,24},{1,5},{5... | collective-permute-start | bytes 5505032 | tf_op jit(solution)/shard_map/ppermute | solution.py:35
  118.2 41.1 %collective-permute-start.7 = (bf16[448,2048]{1,0:T(8,128)(2,1)}, bf16[448,2048]{1,0:T(8,128)(2,1)}, u32[]{:S(2)}, u32[]{:S(2)}) collective-permute-start(bf16[448,2048]{1,0:T(8,128)(2,1)} %collective-permute-done.4.refs_3_), channel_id=1, source_target_pairs={{0,4},{4,0},{8,12},{12,8},{16,20},{20,16},{24,28},{28,24},{1,5},{5... | collective-permute-start | bytes 5505032 | tf_op jit(solution)/shard_map/ppermute | solution.py:35
  154.8 2.8 collective-permute-start.10
  156.5 2.8 collective-permute-start.11
  156.6 14.5 %copy-start.18 = (f32[4,896]{1,0:T(4,128)S(1)}, f32[4,896]{1,0:T(4,128)}, u32[]{:S(2)}) copy-start(f32[4,896]{1,0:T(4,128)} %taps_ref.1) | copy-start | bytes 43012
  156.6 14.5 %copy-start.19 = (f32[4,128]{1,0:T(4,128)S(1)}, f32[4,128]{1,0:T(4,128)}, u32[]{:S(2)}) copy-start(f32[4,128]{1,0:T(4,128)} %bc_taps_ref.1) | copy-start | bytes 6148
  178.3 19.0 %collective-permute-start.12 = (bf16[384,896]{1,0:T(8,128)(2,1)S(1)}, bf16[384,896]{1,0:T(8,128)(2,1)S(1)}, u32[]{:S(2)}, u32[]{:S(2)}) collective-permute-start(bf16[384,896]{1,0:T(8,128)(2,1)S(1)} %get-tuple-element.69.refs_0_), channel_id=1, source_target_pairs={{0,1},{1,2},{2,3},{4,5},{5,6},{6,7},{8,9},{9,10},{10,11},{12,13},{... | collective-permute-start | bytes 2064392 | tf_op jit(solution)/shard_map/ppermute | solution.py:138
  182.3 19.2 %collective-permute-start.13 = (bf16[384,896]{1,0:T(8,128)(2,1)S(1)}, bf16[384,896]{1,0:T(8,128)(2,1)}, u32[]{:S(2)}, u32[]{:S(2)}) collective-permute-start(bf16[384,896]{1,0:T(8,128)(2,1)S(1)} %get-tuple-element.69.refs_0_), channel_id=1, source_target_pairs={{1,0},{2,1},{3,2},{5,4},{6,5},{7,6},{9,8},{10,9},{11,10},{13,12},{... | collective-permute-start | bytes 2064392 | tf_op jit(solution)/shard_map/ppermute | solution.py:139
  201.6 174.6 %all-gather.11.cloned.1.call-start = ((), (), s32[]{:S(2)}) async-start(), calls=%async_computation.5 | async-start | bytes 7225344 | tf_op jit(solution)/shard_map/all_gather | solution.py:195
  201.6 17.2 %collective-permute-start.14 = (bf16[384,896]{1,0:T(8,128)(2,1)S(1)}, bf16[384,896]{1,0:T(8,128)(2,1)S(1)}, u32[]{:S(2)}, u32[]{:S(2)}) collective-permute-start(bf16[384,896]{1,0:T(8,128)(2,1)S(1)} %collective-permute-done.12.refs_3_), channel_id=1, source_target_pairs={{0,1},{1,2},{2,3},{4,5},{5,6},{6,7},{8,9},{9,10},{10,11},{12,13},{... | collective-permute-start | bytes 2064392 | tf_op jit(solution)/shard_map/ppermute | solution.py:138
  205.1 18.2 %collective-permute-start.15 = (bf16[384,896]{1,0:T(8,128)(2,1)}, bf16[384,896]{1,0:T(8,128)(2,1)S(1)}, u32[]{:S(2)}, u32[]{:S(2)}) collective-permute-start(bf16[384,896]{1,0:T(8,128)(2,1)} %collective-permute-done.13.refs_6_), channel_id=1, source_target_pairs={{1,0},{2,1},{3,2},{5,4},{6,5},{7,6},{9,8},{10,9},{11,10},{13,12},{... | collective-permute-start | bytes 2064392 | tf_op jit(solution)/shard_map/ppermute | solution.py:139
  223.2 15.9 %collective-permute-start.16 = (bf16[384,896]{1,0:T(8,128)(2,1)S(1)}, bf16[384,896]{1,0:T(8,128)(2,1)S(1)}, u32[]{:S(2)}, u32[]{:S(2)}) collective-permute-start(bf16[384,896]{1,0:T(8,128)(2,1)S(1)} %collective-permute-done.14.refs_0_), channel_id=1, source_target_pairs={{0,1},{1,2},{2,3},{4,5},{5,6},{6,7},{8,9},{9,10},{10,11},{12,13},{... | collective-permute-start | bytes 2064392 | tf_op jit(solution)/shard_map/ppermute | solution.py:138
  226.4 16.8 %collective-permute-start.17 = (bf16[384,896]{1,0:T(8,128)(2,1)S(1)}, bf16[384,896]{1,0:T(8,128)(2,1)S(1)}, u32[]{:S(2)}, u32[]{:S(2)}) collective-permute-start(bf16[384,896]{1,0:T(8,128)(2,1)S(1)} %collective-permute-done.15.refs_3_), channel_id=1, source_target_pairs={{1,0},{2,1},{3,2},{5,4},{6,5},{7,6},{9,8},{10,9},{11,10},{13,12},{... | collective-permute-start | bytes 2064392 | tf_op jit(solution)/shard_map/ppermute | solution.py:139
  248.2 16.0 %collective-permute-start.19 = (bf16[896,384]{1,0:T(8,128)(2,1)S(1)}, bf16[896,384]{1,0:T(8,128)(2,1)S(1)}, u32[]{:S(2)}, u32[]{:S(2)}) collective-permute-start(bf16[896,384]{1,0:T(8,128)(2,1)S(1)} %far_mixer.1.refs_5_), channel_id=1, source_target_pairs={{1,0},{2,1},{3,2},{5,4},{6,5},{7,6},{9,8},{10,9},{11,10},{13,12},{... | collective-permute-start | bytes 2064392 | tf_op jit(solution)/shard_map/ppermute | solution.py:139
  249.5 16.0 %collective-permute-start.18 = (bf16[896,384]{1,0:T(8,128)(2,1)S(1)}, bf16[896,384]{1,0:T(8,128)(2,1)S(1)}, u32[]{:S(2)}, u32[]{:S(2)}) collective-permute-start(bf16[896,384]{1,0:T(8,128)(2,1)S(1)} %far_mixer.1.refs_5_), channel_id=1, source_target_pairs={{0,1},{1,2},{2,3},{4,5},{5,6},{6,7},{8,9},{9,10},{10,11},{12,13},{... | collective-permute-start | bytes 2064392 | tf_op jit(solution)/shard_map/ppermute | solution.py:138
  264.2 15.5 %collective-permute-start.20 = (bf16[896,384]{1,0:T(8,128)(2,1)S(1)}, bf16[896,384]{1,0:T(8,128)(2,1)S(1)}, u32[]{:S(2)}, u32[]{:S(2)}) collective-permute-start(bf16[896,384]{1,0:T(8,128)(2,1)S(1)} %collective-permute-done.19), channel_id=1, source_target_pairs={{1,0},{2,1},{3,2},{5,4},{6,5},{7,6},{9,8},{10,9},{11,10},{13,12},{... | collective-permute-start | bytes 2064392 | tf_op jit(solution)/shard_map/ppermute | solution.py:139
  265.5 15.6 %collective-permute-start.22 = (bf16[896,384]{1,0:T(8,128)(2,1)S(1)}, bf16[896,384]{1,0:T(8,128)(2,1)S(1)}, u32[]{:S(2)}, u32[]{:S(2)}) collective-permute-start(bf16[896,384]{1,0:T(8,128)(2,1)S(1)} %collective-permute-done.18), channel_id=1, source_target_pairs={{0,1},{1,2},{2,3},{4,5},{5,6},{6,7},{8,9},{9,10},{10,11},{12,13},{... | collective-permute-start | bytes 2064392 | tf_op jit(solution)/shard_map/ppermute | solution.py:138
  279.7 14.6 %collective-permute-start.21 = (bf16[896,384]{1,0:T(8,128)(2,1)S(1)}, bf16[896,384]{1,0:T(8,128)(2,1)}, u32[]{:S(2)}, u32[]{:S(2)}) collective-permute-start(bf16[896,384]{1,0:T(8,128)(2,1)S(1)} %collective-permute-done.20), channel_id=1, source_target_pairs={{1,0},{2,1},{3,2},{5,4},{6,5},{7,6},{9,8},{10,9},{11,10},{13,12},{... | collective-permute-start | bytes 2064392 | tf_op jit(solution)/shard_map/ppermute | solution.py:139
  281.1 14.7 %collective-permute-start.23 = (bf16[896,384]{1,0:T(8,128)(2,1)S(1)}, bf16[896,384]{1,0:T(8,128)(2,1)S(1)}, u32[]{:S(2)}, u32[]{:S(2)}) collective-permute-start(bf16[896,384]{1,0:T(8,128)(2,1)S(1)} %collective-permute-done.22), channel_id=1, source_target_pairs={{0,1},{1,2},{2,3},{4,5},{5,6},{6,7},{8,9},{9,10},{10,11},{12,13},{... | collective-permute-start | bytes 2064392 | tf_op jit(solution)/shard_map/ppermute | solution.py:138
  328.3 17.3 %copy-start.13 = (bf16[384,896]{1,0:T(8,128)(2,1)S(1)}, bf16[384,896]{1,0:T(8,128)(2,1)}, u32[]{:S(2)}) copy-start(bf16[384,896]{1,0:T(8,128)(2,1)} %qkv.2.q_ref) | copy-start | bytes 2064388
  349.2 18.4 %collective-permute-start.24 = (bf16[384,896]{1,0:T(8,128)(2,1)S(1)}, bf16[384,896]{1,0:T(8,128)(2,1)}, u32[]{:S(2)}, u32[]{:S(2)}) collective-permute-start(bf16[384,896]{1,0:T(8,128)(2,1)S(1)} %attend.1.refs_0_), channel_id=1, source_target_pairs={{0,1},{1,2},{2,3},{4,5},{5,6},{6,7},{8,9},{9,10},{10,11},{12,13},{... | collective-permute-start | bytes 2064392 | tf_op jit(solution)/shard_map/ppermute | solution.py:138
  353.4 19.6 %collective-permute-start.26 = (bf16[384,896]{1,0:T(8,128)(2,1)S(1)}, bf16[384,896]{1,0:T(8,128)(2,1)}, u32[]{:S(2)}, u32[]{:S(2)}) collective-permute-start(bf16[384,896]{1,0:T(8,128)(2,1)S(1)} %attend.1.refs_0_), channel_id=1, source_target_pairs={{1,0},{2,1},{3,2},{5,4},{6,5},{7,6},{9,8},{10,9},{11,10},{13,12},{... | collective-permute-start | bytes 2064392 | tf_op jit(solution)/shard_map/ppermute | solution.py:139
  367.7 19.1 %collective-permute-start.25 = (bf16[384,896]{1,0:T(8,128)(2,1)}, bf16[384,896]{1,0:T(8,128)(2,1)}, u32[]{:S(2)}, u32[]{:S(2)}) collective-permute-start(bf16[384,896]{1,0:T(8,128)(2,1)} %collective-permute-done.24.refs_2_), channel_id=1, source_target_pairs={{0,1},{1,2},{2,3},{4,5},{5,6},{6,7},{8,9},{9,10},{10,11},{12,13},{... | collective-permute-start | bytes 2064392 | tf_op jit(solution)/shard_map/ppermute | solution.py:138
  373.0 18.7 %collective-permute-start.27 = (bf16[384,896]{1,0:T(8,128)(2,1)}, bf16[384,896]{1,0:T(8,128)(2,1)}, u32[]{:S(2)}, u32[]{:S(2)}) collective-permute-start(bf16[384,896]{1,0:T(8,128)(2,1)} %collective-permute-done.26.refs_4_), channel_id=1, source_target_pairs={{1,0},{2,1},{3,2},{5,4},{6,5},{7,6},{9,8},{10,9},{11,10},{13,12},{... | collective-permute-start | bytes 2064392 | tf_op jit(solution)/shard_map/ppermute | solution.py:139
  391.7 16.0 %collective-permute-start.28 = (bf16[384,896]{1,0:T(8,128)(2,1)}, bf16[384,896]{1,0:T(8,128)(2,1)}, u32[]{:S(2)}, u32[]{:S(2)}) collective-permute-start(bf16[384,896]{1,0:T(8,128)(2,1)} %collective-permute-done.25.refs_0_), channel_id=1, source_target_pairs={{0,1},{1,2},{2,3},{4,5},{5,6},{6,7},{8,9},{9,10},{10,11},{12,13},{... | collective-permute-start | bytes 2064392 | tf_op jit(solution)/shard_map/ppermute | solution.py:138
  395.1 17.5 %collective-permute-start.29 = (bf16[384,896]{1,0:T(8,128)(2,1)}, bf16[384,896]{1,0:T(8,128)(2,1)}, u32[]{:S(2)}, u32[]{:S(2)}) collective-permute-start(bf16[384,896]{1,0:T(8,128)(2,1)} %collective-permute-done.27.refs_2_), channel_id=1, source_target_pairs={{1,0},{2,1},{3,2},{5,4},{6,5},{7,6},{9,8},{10,9},{11,10},{13,12},{... | collective-permute-start | bytes 2064392 | tf_op jit(solution)/shard_map/ppermute | solution.py:139
  402.8 20.0 %copy-start.15 = (f32[896,64]{1,0:T(8,128)S(1)}, f32[896,64]{1,0:T(8,128)}, u32[]{:S(2)}) copy-start(f32[896,64]{1,0:T(8,128)} %copy-done.14) | copy-start | bytes 688132
  402.8 20.0 %copy-start.21 = (f32[1,14,64,64]{3,2,1,0:T(8,128)S(1)}, f32[1,14,64,64]{3,2,1,0:T(8,128)}, u32[]{:S(2)}) copy-start(f32[1,14,64,64]{3,2,1,0:T(8,128)} %param.26) | copy-start | bytes 688132
  412.7 21.2 %copy-start.1 = (bf16[4,128,3,896]{3,1,2,0:T(8,128)(2,1)S(1)}, bf16[4,128,3,896]{3,1,2,0:T(8,128)(2,1)}, u32[]{:S(2)}) copy-start(bf16[4,128,3,896]{3,1,2,0:T(8,128)(2,1)} %param.40) | copy-start | bytes 8257540
  418.3 8.7 %collective-permute-start.30 = (bf16[224,384]{1,0:T(8,128)(2,1)S(1)}, bf16[224,384]{1,0:T(8,128)(2,1)S(1)}, u32[]{:S(2)}, u32[]{:S(2)}) collective-permute-start(bf16[224,384]{1,0:T(8,128)(2,1)S(1)} %get-tuple-element.102), channel_id=1, source_target_pairs={{0,1},{1,0},{2,3},{3,2},{4,5},{5,4},{6,7},{7,6},{8,9},{9,8},{10,11... | collective-permute-start | bytes 516104 | tf_op jit(solution)/shard_map/ppermute | solution.py:35
  419.0 13.1 %collective-permute-start.31 = (bf16[224,384]{1,0:T(8,128)(2,1)S(1)}, bf16[224,384]{1,0:T(8,128)(2,1)S(1)}, u32[]{:S(2)}, u32[]{:S(2)}) collective-permute-start(bf16[224,384]{1,0:T(8,128)(2,1)S(1)} %get-tuple-element.101), channel_id=1, source_target_pairs={{0,2},{1,3},{2,0},{3,1},{4,6},{5,7},{6,4},{7,5},{8,10},{9,11},{10,... | collective-permute-start | bytes 516104 | tf_op jit(solution)/shard_map/ppermute | solution.py:35
  419.0 13.1 %collective-permute-start.32 = (bf16[224,384]{1,0:T(8,128)(2,1)S(1)}, bf16[224,384]{1,0:T(8,128)(2,1)S(1)}, u32[]{:S(2)}, u32[]{:S(2)}) collective-permute-start(bf16[224,384]{1,0:T(8,128)(2,1)S(1)} %get-tuple-element.100), channel_id=1, source_target_pairs={{0,3},{1,2},{2,1},{3,0},{4,7},{5,6},{6,5},{7,4},{8,11},{9,10},{10,... | collective-permute-start | bytes 516104 | tf_op jit(solution)/shard_map/ppermute | solution.py:35
  (19 other events, 44.5 us)
Sparse Core Ops, SparseCore 0:
  10.0 48.7 all-gather.4
  108.1 90.6 all-gather.6
  201.7 126.5 all-gather.8
  330.0 46.0 all-gather.10
